TPU v7x, 256 devices: a whole 4x4x8 slice. The times are simulated.
256 devices in a mesh: tm: 32 (over x, z), dp: 8 (over y, core).
Axes of the slice: x: 4, y: 4, z: 8, core: 2. Of those that a mesh axis runs over, the one named last changes fastest.
Arguments:
- video: bfloat16 [8, 64, 16, 64, 128], P('dp', 'tm')
- clip_first: int32 [8, 64], P('dp', 'tm'), may hold values from 0 to 63, as said below
- kernel: bfloat16 [3, 3, 3, 128, 128], replicated, may hold values from -0.109375 to 0.109375
- bias: float32 [128], replicated, may hold values from -3 to 3
- cotangent: bfloat16 [8, 64, 8, 32, 128], P('dp', 'tm'), may hold values from -6 to 6
Outputs:
- downsampled: bfloat16 [8, 64, 8, 32, 128], P('dp', 'tm')
- kernel_grad: float32 [3, 3, 3, 128, 128], replicated
Inputs may be any that keep to these rules, and one draw needn't show every extreme that they name: `clip_first`: frames of one clip share the index of the clip's first frame; it never falls along a stream and is at most the frame's own index. Every stream holds at least two clips. Clips are 17 to 121 frames long, the first one of a stream cut off at its start and the last one at its end.
All inputs are finite; a program needn't handle non-finite values.
Results may differ from a plain program's by a relative error of at most 0.02.
Values may be sent and summed in bfloat16 or wider, within the bound.
A program may use at most 64 MiB of HBM per device.

v0:
```python
import jax
import jax.numpy as jnp
from jax import lax
from jax.sharding import PartitionSpec as P


def prefix(part, axis, combine, identity):
    place = lax.axis_index(axis)
    gathered = jax.tree.map(lambda a: lax.all_gather(a, axis), part)
    state = jax.tree.map(lambda a, e: jnp.zeros_like(a) + jnp.asarray(e, a.dtype), part, identity)

    def one(hop, state):
        return combine(
            state, jax.tree.map(lambda a: lax.dynamic_index_in_dim(a, hop, 0, False), gathered)
        )

    return lax.fori_loop(0, place, one, state)


def shifted(block, axis, distance):
    devices = range(lax.axis_size(axis))
    route = [(i - distance, i) for i in devices if i - distance in devices]
    return lax.ppermute(block, axis, route)


def slope(value):
    logistic = jax.nn.sigmoid(value)
    return logistic * (1.0 + value * (1.0 - logistic))


def conv_taps(padded, valid, kernel, bias):
    frames = valid.shape[0]
    height = padded.shape[1] - 2
    width = padded.shape[2] - 2
    chans = padded.shape[3]
    total = jnp.zeros((frames * height * width, chans), jnp.float32)
    for step in range(3):
        part = jnp.zeros((frames * height * width, chans), jnp.float32)
        for row_off in range(3):
            for col_off in range(3):
                piece = padded[
                    step : step + frames, row_off : row_off + height, col_off : col_off + width
                ].reshape(-1, chans)
                part = part + jnp.dot(
                    piece, kernel[step, row_off, col_off], preferred_element_type=jnp.float32
                )
        weight = jnp.repeat(valid[:, step], height * width)
        total = total + part * weight[:, None]
    return total + bias[None, :]


def tap_grads(padded, valid, dconv):
    frames = valid.shape[0]
    height = padded.shape[1] - 2
    width = padded.shape[2] - 2
    chans = padded.shape[3]
    shaped = dconv.reshape(frames, height * width, chans)
    result = []
    for step in range(3):
        masked = (shaped * valid[:, step][:, None, None].astype(jnp.bfloat16)).reshape(-1, chans)
        for row_off in range(3):
            for col_off in range(3):
                piece = padded[
                    step : step + frames, row_off : row_off + height, col_off : col_off + width
                ].reshape(-1, chans)
                result.append(
                    lax.dot_general(
                        piece, masked, (((0,), (0,)), ((), ())), preferred_element_type=jnp.float32
                    )
                )
    return jnp.stack(result).reshape(3, 3, 3, chans, chans)


def join_stats(earlier, later):
    early_last, early_sums, early_count = earlier
    late_last, late_sums, late_count = later
    present = late_last >= 0.0
    same_clip = late_last == early_last
    sums = jnp.where(present, jnp.where(same_clip, early_sums + late_sums, late_sums), early_sums)
    count = jnp.where(
        present, jnp.where(same_clip, early_count + late_count, late_count), early_count
    )
    last = jnp.where(present, late_last, early_last)
    return (last, sums, count)


def per_device(video, clip_first, kernel, bias, cotangent):
    frames_in = video[0]
    first = clip_first[0]
    frames, height, width, chans = frames_in.shape
    groups = chans // 4
    anchor = lax.axis_index("tm") * frames
    grouped = frames_in.astype(jnp.float32).reshape(frames, height * width, groups, 4)
    frame_sums = jnp.stack(
        [jnp.sum(grouped, axis=(1, 3)), jnp.sum(grouped * grouped, axis=(1, 3))], 1
    )
    place = jnp.arange(frames, dtype=jnp.int32)
    member = ((first[None, :] == first[:, None]) & (place[None, :] <= place[:, None])).astype(
        jnp.float32
    )
    local_sums = jnp.einsum("ts,sjg->tjg", member, frame_sums, precision=lax.Precision.HIGHEST)
    local_count = jnp.sum(member, axis=1)
    trailing = (first == first[frames - 1]).astype(jnp.float32)
    tail_last = first[frames - 1 :].astype(jnp.float32)
    tail_sums = jnp.einsum("s,sjg->jg", trailing, frame_sums, precision=lax.Precision.HIGHEST)
    tail_count = jnp.sum(trailing)[None]
    blank = (
        jnp.full((1,), -1.0, jnp.float32),
        jnp.zeros((2, groups), jnp.float32),
        jnp.zeros((1,), jnp.float32),
    )
    prior_last, prior_sums, prior_count = prefix(
        (tail_last, tail_sums, tail_count), "tm", join_stats, blank
    )
    carried = (first.astype(jnp.float32) == prior_last[0]).astype(jnp.float32)
    sums = local_sums + carried[:, None, None] * prior_sums[None]
    count = (local_count + carried * prior_count[0]) * (height * width * 4)
    mean = sums[:, 0] / count[:, None]
    var = sums[:, 1] / count[:, None] - mean * mean
    scale = lax.rsqrt(var + 1e-05)
    normed = (
        ((grouped - mean[:, None, :, None]) * scale[:, None, :, None])
        .reshape(frames_in.shape)
        .astype(jnp.bfloat16)
    )
    rim = shifted(normed, "tm", 1)
    extended = jnp.concatenate([rim, normed], 0)
    padded = jnp.pad(extended, ((0, 0), (1, 1), (1, 1), (0, 0)))
    global_place = anchor + place
    valid = (
        global_place[:, None] - 2 + jnp.arange(3, dtype=jnp.int32)[None, :] >= first[:, None]
    ).astype(jnp.float32)
    conv = conv_taps(padded, valid, kernel, bias)
    active = jax.nn.silu(conv).reshape(frames, height // 2, 2, width // 2, 2, chans)
    output = jnp.mean(active, axis=(2, 4)).astype(jnp.bfloat16)
    spread = jnp.broadcast_to(
        cotangent[0].astype(jnp.float32)[:, :, None, :, None, :] * 0.25,
        (frames, height // 2, 2, width // 2, 2, chans),
    )
    dconv = (spread.reshape(-1, chans) * slope(conv)).astype(jnp.bfloat16)
    terms = tap_grads(padded, valid, dconv)
    total = lax.psum(terms, ("tm", "dp"))
    return (output[None], total)


def solution(mesh):
    in_specs = (
        P("dp", "tm", None, None, None),
        P("dp", "tm"),
        P(),
        P(),
        P("dp", "tm", None, None, None),
    )
    out_specs = (P("dp", "tm", None, None, None), P())
    return jax.shard_map(
        per_device, mesh=mesh, in_specs=in_specs, out_specs=out_specs, check_vma=False
    )
```

profile of v0, /device:TPU:1, one launch (start us, length us, event | category | flops | bytes accessed | tf_op | source)
XLA Modules:
  0.0 564.6 jit_solution(13720896509658883179)
XLA Ops:
  7.2 1.3 slice.211
  9.2 1.9 fusion.105
  11.1 1.2 convert_reduce_fusion
  12.8 1.4 fusion.101
  14.2 36.7 %all-gather.1 = f32[32,2,32]{2,1,0:T(2,128)S(1)} all-gather(f32[1,2,32]{2,1,0:T(2,128)S(1)} %bitcast.487), channel_id=2, replica_groups=mesh['tm'=32,'dp'=8] {'tm'}, dimensions={0}, use_global_device_ids=true | all-gather | bytes 8448 | tf_op jit(solution)/shard_map/all_gather | solution.py:9
  50.9 1.3 dynamic-slice
  52.2 0.7 bitcast_dynamic-update-slice_fusion
  52.9 1.4 dynamic-update-slice.1
  54.3 58.1 %all-reduce.3 = (f32[32]{0:T(128)S(1)}, f32[32]{0:T(128)S(1)}) all-reduce(f32[32]{0:T(128)S(1)} %bitcast_dynamic-update-slice_fusion, f32[32]{0:T(128)S(1)} %dynamic-update-slice.1), channel_id=1, replica_groups=mesh['tm'=32,'dp'=8] {'tm'}, use_global_device_ids=true, to_apply=%add.1 | all-reduce | flops 64 | bytes 512
  112.4 0.7 compare_convert_fusion
  113.0 0.9 convert_reduce_fusion.1
  113.9 0.9 convolution_add_fusion.23
  114.9 0.7 fusion.107
  116.2 4.8 collective-permute-start
  121.6 5.5 collective-permute-done
  127.2 3.9 pad_slice_fusion.2
  131.1 0.9 pad_slice_fusion.3
  132.0 0.3 copy-done.2
  133.1 0.3 fusion.49
  133.4 0.3 convolution_add_fusion.22
  134.0 0.3 convolution_add_fusion.20
  134.3 0.3 fusion.7
  134.6 0.3 convolution_add_fusion.18
  135.4 0.3 convolution_add_fusion.14
  136.6 0.3 convolution_add_fusion.10
  137.2 0.3 convolution_add_fusion.7
  138.0 0.3 convolution_add_fusion.4
  138.9 0.3 convolution_add_fusion.1
  139.2 0.4 fusion.6
  139.6 0.4 fusion.5
  140.0 0.5 broadcast_in_dim.47
  140.4 1.7 multiply_convert_fusion
  142.1 0.6 fusion.34
  142.8 0.6 fusion.33
  143.4 0.6 fusion.32
  144.0 0.6 fusion.31
  144.7 0.6 fusion.30
  145.3 0.6 fusion.29
  145.9 0.6 fusion.28
  146.5 0.6 fusion.27
  147.2 0.6 fusion.26
  147.8 0.8 fusion.25
  148.6 0.6 fusion.24
  149.3 0.6 fusion.23
  149.9 0.6 fusion.22
  150.5 0.6 fusion.21
  151.2 0.6 fusion.20
  151.8 0.6 fusion.19
  152.4 0.6 fusion.18
  153.0 0.6 fusion.17
  153.7 0.6 fusion.16
  154.3 0.6 fusion.15
  154.9 0.6 fusion.14
  155.6 0.6 fusion.13
  156.2 0.6 fusion.12
  156.8 0.6 fusion.11
  157.5 0.6 fusion.10
  158.1 0.6 fusion.9
  158.7 0.6 fusion.8
  159.4 1.2 copy-done.1
  160.6 2.0 reduce_sum.67
  162.6 0.7 fusion.40
  163.3 391.6 %all-reduce.6.cloned.1.call-done = f32[3,3,3,128,128]{4,3,2,1,0:T(8,128)} async-done(((f32[3,3,3,128,128]{4,3,2,1,0:T(8,128)}), f32[3,3,3,128,128]{4,3,2,1,0:T(8,128)}) %all-reduce.6.cloned.1.call-update) | async-done | bytes 1769488 | tf_op jit(solution)/shard_map/psum | solution.py:142
  554.9 2.9 copy.72
  (58 shorter events, 5.6 us)
Async XLA Ops:
  7.2 113.8 %copy-start.4 = (s32[1,2]{1,0:T(1,128)S(1)}, s32[1,2]{1,0:T(1,128)}, u32[]{:S(2)}) copy-start(s32[1,2]{1,0:T(1,128)} %param.8) | copy-start | bytes 28
  7.2 108.8 %copy-start = (bf16[1,2,16,64,128]{4,3,2,1,0:T(8,128)(2,1)S(1)}, bf16[1,2,16,64,128]{4,3,2,1,0:T(8,128)(2,1)}, u32[]{:S(2)}) copy-start(bf16[1,2,16,64,128]{4,3,2,1,0:T(8,128)(2,1)} %param.7) | copy-start | bytes 1572868
  7.2 547.7 %all-reduce.6.cloned.1.call-start = ((), (), s32[]{:S(2)}) async-start(), calls=%async_computation | async-start | bytes 3538944 | tf_op jit(solution)/shard_map/psum | solution.py:142
  11.1 110.4 %copy-start.3 = (bf16[1,2,8,32,128]{4,3,2,1,0:T(8,128)(2,1)S(1)}, bf16[1,2,8,32,128]{4,3,2,1,0:T(8,128)(2,1)}, u32[]{:S(2)}) copy-start(bf16[1,2,8,32,128]{4,3,2,1,0:T(8,128)(2,1)} %param.11) | copy-start | bytes 393220
  116.2 10.9 %collective-permute-start = (bf16[2,16,64,128]{3,2,1,0:T(8,128)(2,1)S(1)}, bf16[2,16,64,128]{3,2,1,0:T(8,128)(2,1)S(1)}, u32[]{:S(2)}, u32[]{:S(2)}) collective-permute-start(bf16[2,16,64,128]{3,2,1,0:T(8,128)(2,1)S(1)} %fusion.37), channel_id=1, source_target_pairs={{0,8},{8,16},{16,24},{24,32},{32,40},{40,48},{48,56},{56,64},{64,7... | collective-permute-start | bytes 1572872 | tf_op jit(solution)/shard_map/ppermute | solution.py:23
  131.1 1.2 copy-start.2
  139.6 0.9 copy-start.5
  159.4 1.2 copy-start.1
Sparse Core Ops, SparseCore 0:
  160.7 394.1 all-reduce.5
where the time goes:
time: 568 us; the launch traced here: 565 us
  waiting for transfers between devices  397 us (70%)
  blocking collectives  94.8 us (17%)
  matrix products  28.6 us (5%)
  local copies, waits for them, and re-layouts  15.3 us (3%)
  between operations  15.2 us (3%)
  other arithmetic  8.82 us (2%)
    psum x1, waiting for transfers between devices, per_device(): total = lax.psum(terms, ('tm', 'dp'))  392 us
    unnamed x1, blocking collectives  58.1 us
    all_gather x1, blocking collectives, prefix(): gathered = jax.tree.map(lambda a: lax.all_gather(a, axis), part)  36.7 us
    dot_general x27, matrix products, tap_grads(): lax.dot_general(piece, masked, (((0,), (0,)), ((), ())), preferred_elemen...  17.1 us
  transfers between devices with their start and end apart: 2, of which 2 were waited for; matrix products, arithmetic and copies ran while one was open for 1% of the time, Pallas kernels for 0%

commit v1 on v0

v1 whole, which is shorter than its diff:
```python
import functools

import jax
import jax.numpy as jnp
from jax import lax
from jax.experimental import pallas as pl
from jax.experimental.pallas import tpu as pltpu
from jax.sharding import PartitionSpec as P

F32 = jnp.float32
BF16 = jnp.bfloat16
TILES = 27 * 4


def fused(
    nx,
    nz,
    ny,
    first_ref,
    bias_ref,
    video_hbm,
    kern_hbm,
    cot_hbm,
    down_ref,
    grad_hbm,
    vid,
    halo,
    kern,
    cot,
    xs,
    acc,
    spread,
    pool,
    dts,
    dtm,
    gath,
    grads,
    r_pair,
    part,
    r_plane,
    a32,
    a16,
    r_z,
    full,
    local_sem,
    halo_send,
    halo_recv,
    stat_send,
    stat_recv,
    pair_send,
    pair_recv,
    plane_send,
    plane_recv,
    z_send,
    z_recv,
    zg_send,
    zg_recv,
    pg_send,
    pg_recv,
    cg_send,
    cg_recv,
):
    _, frames, height, width, chans = video_hbm.shape
    half_h, half_w = height // 2, width // 2
    pixels = height * width
    n_plane = nx * ny
    n_tm = nx * nz
    slots = grads.shape[2]
    used = r_pair.shape[1]
    zt = slots // nz

    tm = lax.axis_index("tm")
    dp = lax.axis_index("dp")
    x, z = tm // nz, tm % nz
    y, core = dp // 2, dp % 2
    plane = x * ny + y

    def at(tm_to, dp_to):
        return {"tm": tm_to, "dp": dp_to}

    def plane_peer(q):
        return at((q // ny) * nz + z, (q % ny) * 2 + core)

    def z_peer(q):
        return at(x * nz + q, dp)

    sibling = at(tm, y * 2 + 1 - core)

    def remote(src, dst, send, recv, to):
        return pltpu.make_async_remote_copy(
            src_ref=src,
            dst_ref=dst,
            send_sem=send,
            recv_sem=recv,
            device_id=to,
            device_id_type=pl.DeviceIdType.MESH,
        )

    loads = [
        pltpu.make_async_copy(video_hbm.at[0], vid, local_sem.at[0]),
        pltpu.make_async_copy(cot_hbm.at[0], cot, local_sem.at[1]),
        pltpu.make_async_copy(kern_hbm, kern, local_sem.at[2]),
    ]
    for load in loads:
        load.start()

    barrier = pltpu.get_barrier_semaphore()
    peers = [sibling]
    peers += [at((tm + d) % n_tm, dp) for d in range(1, n_tm)]
    for d in range(1, n_plane):
        q = (plane + d) % n_plane
        peers.append(plane_peer(q))
    for peer in peers:
        pl.semaphore_signal(barrier, inc=1, device_id=peer, device_id_type=pl.DeviceIdType.MESH)

    loads[0].wait()
    rows = []
    for f in range(frames):
        value = vid[f].astype(F32)
        rows.append(jnp.sum(jnp.sum(value, axis=0), axis=0, keepdims=True))
        rows.append(jnp.sum(jnp.sum(value * value, axis=0), axis=0, keepdims=True))
    rows.append(jnp.zeros((4, chans), F32))
    stat = jnp.concatenate(rows, axis=0)
    lane = lax.broadcasted_iota(jnp.int32, (8, chans), 1)
    stat = stat + jnp.where(lane % 2 == 0, pltpu.roll(stat, chans - 1, 1), pltpu.roll(stat, 1, 1))
    stat = stat + jnp.where(lane % 4 < 2, pltpu.roll(stat, chans - 2, 1), pltpu.roll(stat, 2, 1))
    gath[tm] = stat

    pl.semaphore_wait(barrier, len(peers))

    following = at((tm + 1) % n_tm, dp)
    halos = [
        remote(video_hbm.at[0, f], halo.at[f], halo_send.at[f], halo_recv.at[f], following)
        for f in range(frames)
    ]
    stats = []
    for d in range(1, n_tm):
        stats.append(
            remote(
                gath.at[tm],
                gath.at[tm],
                stat_send.at[d],
                stat_recv.at[tm],
                at((tm + d) % n_tm, dp),
            )
        )
    for copy in stats:
        copy.start()
    halos[1].start()
    halos[0].start()

    loads[1].wait()
    for f in range(frames):
        for i in range(half_h):
            quarter = cot[f, i].astype(F32) * 0.25
            spread[f * half_h + i, pl.ds(0, half_w, stride=2), :] = quarter
            spread[f * half_h + i, pl.ds(1, half_w, stride=2), :] = quarter
    rim = jnp.zeros((width, 3 * chans), BF16)
    for s in range(4):
        xs[s, 0] = rim
        xs[s, height + 1] = rim
    blank = jnp.zeros((16, chans), BF16)
    for h in range(2):
        for j in range(TILES, n_plane * used):
            grads[h, j // used, j % used] = blank
    for j in range(used, slots):
        a32[j] = jnp.zeros((16, chans), F32)

    first0 = first_ref[0, 0]
    first1 = first_ref[0, 1]
    t0 = tm * frames
    loads[2].wait()

    for d in range(1, n_tm):
        q = (tm + d) % n_tm
        remote(
            gath.at[tm], gath.at[q], stat_send.at[d], stat_recv.at[q], at(q, dp)
        ).wait_recv()

    gathered = gath[...]
    row = lax.broadcasted_iota(jnp.int32, gathered.shape, 1)
    frame = lax.broadcasted_iota(jnp.int32, gathered.shape, 0) * frames + row // 2

    def moments(first, last):
        chosen = jnp.where((frame >= first) & (frame <= last) & (row < 4), gathered, 0.0)
        total = jnp.sum(chosen, axis=0)
        number = jnp.maximum((last - first + 1) * (pixels * 4), 1)
        count = jnp.full((1, chans), number, jnp.int32).astype(F32)
        mean = (total[0:1] + total[2:3]) / count
        var = (total[1:2] + total[3:4]) / count - mean * mean
        return mean, lax.rsqrt(var + 1e-05)

    col = lax.broadcasted_iota(jnp.int32, (width, chans), 0)

    def place(source, f, slot, mean, scale, keep):
        for r in range(height):
            value = (source[f, r].astype(F32) - mean) * scale
            if keep is not None:
                value = jnp.where(keep, value, 0.0)
            left = jnp.where(col == 0, 0.0, pltpu.roll(value, 1, 0))
            right = jnp.where(col == width - 1, 0.0, pltpu.roll(value, width - 1, 0))
            xs[slot, r + 1, :, 0:chans] = left.astype(BF16)
            xs[slot, r + 1, :, chans : 2 * chans] = value.astype(BF16)
            xs[slot, r + 1, :, 2 * chans : 3 * chans] = right.astype(BF16)

    same = jnp.full((1, chans), first1 <= t0, jnp.bool_).astype(F32)
    block = min(8, height)

    def patches(slot, r):
        parts = [xs[slot, r + dy : r + dy + block].reshape(block * width, 3 * chans) for dy in range(3)]
        return jnp.concatenate(parts, axis=1)

    def taps(k):
        return kern[k].reshape(9 * chans, chans)

    def dot(a, b):
        return jnp.dot(a, b, preferred_element_type=F32)

    place(vid, 0, 2, *moments(first0, t0), None)
    place(vid, 1, 3, *moments(first1, t0 + 1), None)
    for r in range(0, height, block):
        both = dot(patches(2, r), jnp.concatenate([taps(2), taps(1)], axis=1))
        own = dot(patches(3, r), taps(2))
        px = pl.ds(r * width, block * width)
        acc[0, px] = both[:, :chans]
        acc[1, px] = both[:, chans:] * same + own

    keep1 = jnp.full((1, chans), first0 <= t0 - 1, jnp.bool_)
    keep0 = jnp.full((1, chans), first0 <= t0 - 2, jnp.bool_)
    halos[1].wait_recv()
    place(halo, 1, 1, *moments(first0, t0 - 1), keep1)
    for r in range(0, height, block):
        both = dot(patches(1, r), jnp.concatenate([taps(1), taps(0)], axis=1))
        px = pl.ds(r * width, block * width)
        acc[0, px] += both[:, :chans]
        acc[1, px] += both[:, chans:] * same
    halos[0].wait_recv()
    place(halo, 0, 0, *moments(first0, t0 - 2), keep0)
    for r in range(0, height, block):
        px = pl.ds(r * width, block * width)
        acc[0, px] += dot(patches(0, r), taps(0))

    bias = bias_ref[...]
    for f in range(frames):
        for i in range(half_h):
            value = acc[f, i * 2 * width : (i + 1) * 2 * width] + bias
            logistic = 1.0 / (1.0 + jnp.exp(-value))
            active = value * logistic
            pool[f * half_h + i] = active[:width] + active[width:]
            slope = logistic * (1.0 + value * (1.0 - logistic))
            over = spread[f * half_h + i]
            dconv = jnp.concatenate([over, over], axis=0) * slope
            turned = dconv.T
            dts[f * chans : (f + 1) * chans, i * 2 * width : (i + 1) * 2 * width] = turned.astype(BF16)
            if f == 1:
                dtm[:, i * 2 * width : (i + 1) * 2 * width] = (turned * same[0:1, 0:1]).astype(BF16)
    for f in range(frames):
        for i in range(half_h):
            even = pool[f * half_h + i, pl.ds(0, half_w, stride=2), :]
            odd = pool[f * half_h + i, pl.ds(1, half_w, stride=2), :]
            down_ref[0, f, i] = ((even + odd) * 0.25).astype(BF16)

    for dy in range(3):
        shifted = [xs[s, dy : dy + height].reshape(pixels, 3 * chans) for s in range(4)]
        d0 = dts[0:chans]
        d1 = dts[chans : 2 * chans]
        two = jnp.concatenate([d0, dtm[...]], axis=0)
        r0 = dot(d0, shifted[0])
        r1 = dot(two, shifted[1])
        r2 = dot(two, shifted[2])
        r3 = dot(d1, shifted[3])
        sums = [r0 + r1[chans:], r1[:chans] + r2[chans:], r2[:chans] + r3]
        for k in range(3):
            for dx in range(3):
                tile = sums[k][:, dx * chans : (dx + 1) * chans].T.astype(BF16)
                tap = (k * 3 + dy) * 3 + dx
                for h in range(2):
                    for q in range(4):
                        j = tap * 4 + q
                        start = (h * 4 + q) * 16
                        grads[h, j // used, j % used] = tile[start : start + 16]

    swap = remote(grads.at[1 - core, :, pl.ds(0, used)], r_pair, pair_send.at[0], pair_recv.at[0], sibling)
    swap.start()
    swap.wait_recv()
    for o in range(n_plane):
        part[o] = (grads[core, o, 0:used].astype(F32) + r_pair[o].astype(F32)).astype(BF16)

    out_plane = []
    for d in range(1, n_plane):
        q = (plane + d) % n_plane
        out_plane.append(
            remote(part.at[q], r_plane.at[plane], plane_send.at[d], plane_recv.at[plane], plane_peer(q))
        )
    for copy in out_plane:
        copy.start()
    total = part[plane].astype(F32)
    for d in range(1, n_plane):
        q = (plane + n_plane - d) % n_plane
        remote(part.at[q], r_plane.at[q], plane_send.at[d], plane_recv.at[q], plane_peer(q)).wait_recv()
        total = total + r_plane[q].astype(F32)
    a32[0:used] = total
    a16[...] = a32[...].astype(BF16)

    out_z = []
    for d in range(1, nz):
        q = (z + d) % nz
        out_z.append(
            remote(a16.at[pl.ds(q * zt, zt)], r_z.at[z], z_send.at[d], z_recv.at[z], z_peer(q))
        )
    for copy in out_z:
        copy.start()
    total = a32[pl.ds(z * zt, zt)]
    for d in range(1, nz):
        q = (z + nz - d) % nz
        remote(a16.at[pl.ds(0, zt)], r_z.at[q], z_send.at[d], z_recv.at[q], z_peer(q)).wait_recv()
        total = total + r_z[q].astype(F32)
    full[core, plane, pl.ds(z * zt, zt)] = total.astype(BF16)

    mine = full.at[core, plane]
    out_zg = []
    for d in range(1, nz):
        q = (z + d) % nz
        own = mine.at[pl.ds(z * zt, zt)]
        out_zg.append(remote(own, own, zg_send.at[d], zg_recv.at[z], z_peer(q)))
    for copy in out_zg:
        copy.start()
    for d in range(1, nz):
        q = (z + nz - d) % nz
        theirs = mine.at[pl.ds(q * zt, zt)]
        remote(theirs, theirs, zg_send.at[d], zg_recv.at[q], z_peer(q)).wait_recv()

    out_pg = []
    for d in range(1, n_plane):
        q = (plane + d) % n_plane
        own = full.at[core, plane]
        out_pg.append(remote(own, own, pg_send.at[d], pg_recv.at[plane], plane_peer(q)))
    for copy in out_pg:
        copy.start()
    for d in range(1, n_plane):
        q = (plane + n_plane - d) % n_plane
        theirs = full.at[core, q]
        remote(theirs, theirs, pg_send.at[d], pg_recv.at[q], plane_peer(q)).wait_recv()

    give = remote(full.at[core], full.at[core], cg_send.at[0], cg_recv.at[0], sibling)
    give.start()
    keep = pltpu.make_async_copy(full.at[core], grad_hbm.at[core], local_sem.at[3])
    keep.start()
    remote(full.at[1 - core], full.at[1 - core], cg_send.at[0], cg_recv.at[0], sibling).wait_recv()
    take = pltpu.make_async_copy(full.at[1 - core], grad_hbm.at[1 - core], local_sem.at[4])
    take.start()

    for copy in halos + stats + [swap] + out_plane + out_z + out_zg + out_pg + [give]:
        copy.wait_send()
    keep.wait()
    take.wait()


def per_device(nx, nz, ny, video, clip_first, kernel, bias, cotangent):
    _, frames, height, width, chans = video.shape
    half_h, half_w = height // 2, width // 2
    n_plane, n_tm = nx * ny, nx * nz
    used = -(-TILES // n_plane)
    zt = -(-used // nz)
    slots = zt * nz
    any_space = pl.BlockSpec(memory_space=pl.ANY)
    vmem = pl.BlockSpec(memory_space=pltpu.VMEM)
    smem = pl.BlockSpec(memory_space=pltpu.SMEM)
    sem = pltpu.SemaphoreType.DMA
    down, grad = pl.pallas_call(
        functools.partial(fused, nx, nz, ny),
        out_shape=(
            jax.ShapeDtypeStruct(cotangent.shape, BF16),
            jax.ShapeDtypeStruct((2, n_plane, slots, 16, chans), BF16),
        ),
        in_specs=[smem, vmem, any_space, any_space, any_space],
        out_specs=(vmem, any_space),
        scratch_shapes=[
            pltpu.VMEM((frames, height, width, chans), BF16),
            pltpu.VMEM((frames, height, width, chans), BF16),
            pltpu.VMEM((3, 3, 3, chans, chans), BF16),
            pltpu.VMEM((frames, half_h, half_w, chans), BF16),
            pltpu.VMEM((4, height + 2, width, 3 * chans), BF16),
            pltpu.VMEM((frames, height * width, chans), F32),
            pltpu.VMEM((frames * half_h, width, chans), F32),
            pltpu.VMEM((frames * half_h, width, chans), F32),
            pltpu.VMEM((frames * chans, height * width), BF16),
            pltpu.VMEM((chans, height * width), BF16),
            pltpu.VMEM((n_tm, 8, chans), F32),
            pltpu.VMEM((2, n_plane, slots, 16, chans), BF16),
            pltpu.VMEM((n_plane, used, 16, chans), BF16),
            pltpu.VMEM((n_plane, used, 16, chans), BF16),
            pltpu.VMEM((n_plane, used, 16, chans), BF16),
            pltpu.VMEM((slots, 16, chans), F32),
            pltpu.VMEM((slots, 16, chans), BF16),
            pltpu.VMEM((nz, zt, 16, chans), BF16),
            pltpu.VMEM((2, n_plane, slots, 16, chans), BF16),
            sem((5,)),
            sem((2,)),
            sem((2,)),
            sem((n_tm,)),
            sem((n_tm,)),
            sem((1,)),
            sem((1,)),
            sem((n_plane,)),
            sem((n_plane,)),
            sem((nz,)),
            sem((nz,)),
            sem((nz,)),
            sem((nz,)),
            sem((n_plane,)),
            sem((n_plane,)),
            sem((1,)),
            sem((1,)),
        ],
        compiler_params=pltpu.CompilerParams(
            collective_id=0, has_side_effects=True, vmem_limit_bytes=48 * 1024 * 1024
        ),
    )(clip_first, bias.reshape(1, chans), video, kernel, cotangent)
    grad = grad[:, :, :used].reshape(2, n_plane * used, 16, chans)[:, :TILES]
    grad = grad.reshape(2, 27, chans // 2, chans).transpose(1, 0, 2, 3)
    return down, grad.reshape(3, 3, 3, chans, chans).astype(F32)


def solution(mesh):
    n_tm, n_dp = mesh.shape["tm"], mesh.shape["dp"]
    nz = 8 if n_tm == 32 else 2
    in_specs = (
        P("dp", "tm", None, None, None),
        P("dp", "tm"),
        P(),
        P(),
        P("dp", "tm", None, None, None),
    )
    out_specs = (P("dp", "tm", None, None, None), P())
    return jax.shard_map(
        functools.partial(per_device, n_tm // nz, nz, n_dp // 2),
        mesh=mesh,
        in_specs=in_specs,
        out_specs=out_specs,
        check_vma=False,
    )
```

time: 568 us -> 70.8 us (0.12)
  waiting for transfers between devices: 397 us -> 0 us
  blocking collectives: 94.8 us -> 0 us
  Pallas kernels: 0 us -> 62.9 us
  matrix products: 28.6 us -> 0 us
  between operations: 15.2 us -> 0.68 us
  other arithmetic: 8.82 us -> 0.19 us
  local copies, waits for them, and re-layouts: 15.3 us -> 6.8 us
    psum x1 -> x0, waiting for transfers between devices: 392 us -> none  [per_device(): total = lax.psum(terms, ('tm', 'dp'))]
    pallas_call x0 -> x1, Pallas kernels: none -> 62.9 us  [per_device(): pl.pallas_call(functools.partial(fused, nx, nz, ny), out_shape=(jax.Shape...]
    unnamed x1 -> x0, blocking collectives: 58.1 us -> none
    all_gather x1 -> x0, blocking collectives: 36.7 us -> none  [prefix(): gathered = jax.tree.map(lambda a: lax.all_gather(a, axis), part)]
    dot_general x56 -> x0, matrix products: 28.6 us -> none  [the longest x27 17.1 us: tap_grads(): lax.dot_general(piece, masked, (((0,), (0,)), ((), ())), preferred_elemen...]
    reduce_sum x6 -> x0, other arithmetic: 6.26 us -> none  [the longest x1 2.02 us: per_device(): output = jnp.mean(active, axis=(2, 4)).astype(jnp.bfloat16)]
    slice x3 -> x2, local copies, waits for them, and re-layouts: 6.14 us -> 0.32 us  [per_device(): grad = grad[:, :, :used].reshape(2, n_plane * used, 16, chans)[:, :TILES]]
  transfers between devices with their start and end apart: 2 -> 0, of which waited for: 2 -> 0; matrix products, arithmetic and copies ran while one was open for 1% -> 0% of each run, Pallas kernels for 0% -> 0%
where the time goes in v1:
time: 70.8 us; the launch traced here: 70.6 us
  Pallas kernels  62.9 us (89%)
  local copies, waits for them, and re-layouts  6.8 us (10%)
    pallas_call x1, Pallas kernels, per_device(): pl.pallas_call(functools.partial(fused, nx, nz, ny), out_shape=(jax.Shape...  62.9 us
    unnamed x11, local copies, waits for them, and re-layouts  5.07 us

profile of v1, /device:TPU:1, one launch (start us, length us, event | category | flops | bytes accessed | tf_op | source)
XLA Modules:
  0.0 70.6 jit_solution(3242756751001395384)
XLA Ops:
  0.6 0.0 copy-start
  0.6 1.2 %copy-done = bf16[3,3,3,128,128]{4,3,2,1,0:T(8,128)(2,1)S(1)} copy-done((bf16[3,3,3,128,128]{4,3,2,1,0:T(8,128)(2,1)S(1)}, bf16[3,3,3,128,128]{4,3,2,1,0:T(8,128)(2,1)}, u32[]{:S(2)}) %copy-start) | copy-done | bytes 884760
  1.8 0.0 copy-start.1
  1.8 1.0 %copy-done.1 = bf16[1,2,16,64,128]{4,3,2,1,0:T(8,128)(2,1)S(1)} copy-done((bf16[1,2,16,64,128]{4,3,2,1,0:T(8,128)(2,1)S(1)}, bf16[1,2,16,64,128]{4,3,2,1,0:T(8,128)(2,1)}, u32[]{:S(2)}) %copy-start.1) | copy-done | bytes 524312
  2.8 0.0 copy-start.2
  2.8 0.9 %copy-done.2 = bf16[1,2,8,32,128]{4,3,2,1,0:T(8,128)(2,1)S(1)} copy-done((bf16[1,2,8,32,128]{4,3,2,1,0:T(8,128)(2,1)S(1)}, bf16[1,2,8,32,128]{4,3,2,1,0:T(8,128)(2,1)}, u32[]{:S(2)}) %copy-start.2) | copy-done | bytes 131096
  3.7 0.0 copy-start.3
  3.7 0.7 copy-done.3
  4.4 0.0 copy-start.4
  4.4 0.7 copy-done.4
  5.1 62.9 %shard_map.68 = (bf16[1,2,8,32,128]{4,3,2,1,0:T(8,128)(2,1)S(1)}, bf16[2,16,8,16,128]{4,3,2,1,0:T(8,128)(2,1)S(1)}) custom-call(s32[1,2]{1,0:T(1,128)S(1)} %copy-done.3, f32[1,128]{1,0:T(1,128)S(1)} %bitcast.9, bf16[1,2,16,64,128]{4,3,2,1,0:T(8,128)(2,1)S(1)} %copy-done.1, bf16[3,3,3,128,128]{4,3,2,1,0:T(8,128)(2,1)S(1)} %copy-done, ...), custom_call_target="tpu_custom_call" | custom-call | tf_op jit(solution)/shard_map/pallas_call | solution.py:370
  68.0 0.2 slice.6
  68.2 0.2 slice.8
  68.3 0.2 bitcast_convert_fusion
  68.5 1.4 %copy.7 = f32[2,27,64,128]{3,2,0,1:T(8,128)} copy(f32[2,27,64,128]{3,2,1,0:T(8,128)S(1)} %bitcast_convert_fusion) | data formatting | bytes 3538944 | tf_op jit(solution)/shard_map/convert_element_type | solution.py:422
  69.9 0.7 copy.9
Async XLA Ops:
  0.6 1.2 %copy-start = (bf16[3,3,3,128,128]{4,3,2,1,0:T(8,128)(2,1)S(1)}, bf16[3,3,3,128,128]{4,3,2,1,0:T(8,128)(2,1)}, u32[]{:S(2)}) copy-start(bf16[3,3,3,128,128]{4,3,2,1,0:T(8,128)(2,1)} %kern_hbm.1) | copy-start | bytes 2654212
  1.8 1.0 %copy-start.1 = (bf16[1,2,16,64,128]{4,3,2,1,0:T(8,128)(2,1)S(1)}, bf16[1,2,16,64,128]{4,3,2,1,0:T(8,128)(2,1)}, u32[]{:S(2)}) copy-start(bf16[1,2,16,64,128]{4,3,2,1,0:T(8,128)(2,1)} %video_hbm.1) | copy-start | bytes 1572868
  2.8 0.9 %copy-start.2 = (bf16[1,2,8,32,128]{4,3,2,1,0:T(8,128)(2,1)S(1)}, bf16[1,2,8,32,128]{4,3,2,1,0:T(8,128)(2,1)}, u32[]{:S(2)}) copy-start(bf16[1,2,8,32,128]{4,3,2,1,0:T(8,128)(2,1)} %cot_hbm.1) | copy-start | bytes 393220
  3.7 0.7 copy-start.3
  4.4 0.7 copy-start.4

commit v2 on v1

--- a/solution.py
+++ b/solution.py
@@ -9,20 +9,22 @@
 
 F32 = jnp.float32
 BF16 = jnp.bfloat16
-TILES = 27 * 4
+HALF = 14 * 8
 
 
 def fused(
     nx,
     nz,
     ny,
-    first_ref,
-    bias_ref,
+    first_hbm,
+    bias_hbm,
     video_hbm,
     kern_hbm,
     cot_hbm,
     down_ref,
     grad_hbm,
+    first_ref,
+    bias_ref,
     vid,
     halo,
     kern,
@@ -43,6 +45,7 @@
     r_z,
     full,
     local_sem,
+    keep_sem,
     halo_send,
     halo_recv,
     stat_send,
@@ -65,9 +68,8 @@
     pixels = height * width
     n_plane = nx * ny
     n_tm = nx * nz
-    slots = grads.shape[2]
-    used = r_pair.shape[1]
-    zt = slots // nz
+    used = HALF // n_plane
+    zt = -(-used // nz)
 
     tm = lax.axis_index("tm")
     dp = lax.axis_index("dp")
@@ -100,6 +102,8 @@
         pltpu.make_async_copy(video_hbm.at[0], vid, local_sem.at[0]),
         pltpu.make_async_copy(cot_hbm.at[0], cot, local_sem.at[1]),
         pltpu.make_async_copy(kern_hbm, kern, local_sem.at[2]),
+        pltpu.make_async_copy(first_hbm, first_ref, local_sem.at[3]),
+        pltpu.make_async_copy(bias_hbm, bias_ref, local_sem.at[4]),
     ]
     for load in loads:
         load.start()
@@ -160,12 +164,11 @@
         xs[s, 0] = rim
         xs[s, height + 1] = rim
     blank = jnp.zeros((16, chans), BF16)
-    for h in range(2):
-        for j in range(TILES, n_plane * used):
-            grads[h, j // used, j % used] = blank
-    for j in range(used, slots):
-        a32[j] = jnp.zeros((16, chans), F32)
-
+    for j in range(27 * 8, 2 * HALF):
+        grads[j] = blank
+
+    loads[3].wait()
+    loads[4].wait()
     first0 = first_ref[0, 0]
     first1 = first_ref[0, 1]
     t0 = tm * frames
@@ -273,109 +276,153 @@
         for k in range(3):
             for dx in range(3):
                 tile = sums[k][:, dx * chans : (dx + 1) * chans].T.astype(BF16)
-                tap = (k * 3 + dy) * 3 + dx
-                for h in range(2):
-                    for q in range(4):
-                        j = tap * 4 + q
-                        start = (h * 4 + q) * 16
-                        grads[h, j // used, j % used] = tile[start : start + 16]
-
-    swap = remote(grads.at[1 - core, :, pl.ds(0, used)], r_pair, pair_send.at[0], pair_recv.at[0], sibling)
+                spot = ((dy * 3 + k) * 3 + dx) * 8
+                for q in range(8):
+                    grads[spot + q] = tile[q * 16 : (q + 1) * 16]
+
+    swap = remote(
+        grads.at[pl.ds((1 - core) * HALF, HALF)], r_pair, pair_send.at[0], pair_recv.at[0], sibling
+    )
     swap.start()
     swap.wait_recv()
     for o in range(n_plane):
-        part[o] = (grads[core, o, 0:used].astype(F32) + r_pair[o].astype(F32)).astype(BF16)
+        tiles = pl.ds(o * used, used)
+        own = grads[pl.ds(core * HALF + o * used, used)].astype(F32)
+        part[tiles] = (own + r_pair[tiles].astype(F32)).astype(BF16)
+
+    def owned(q):
+        return pl.ds(q * used, used)
 
     out_plane = []
     for d in range(1, n_plane):
         q = (plane + d) % n_plane
         out_plane.append(
-            remote(part.at[q], r_plane.at[plane], plane_send.at[d], plane_recv.at[plane], plane_peer(q))
+            remote(
+                part.at[owned(q)], r_plane.at[plane], plane_send.at[d], plane_recv.at[plane], plane_peer(q)
+            )
         )
     for copy in out_plane:
         copy.start()
-    total = part[plane].astype(F32)
+    total = part[owned(plane)].astype(F32)
     for d in range(1, n_plane):
         q = (plane + n_plane - d) % n_plane
-        remote(part.at[q], r_plane.at[q], plane_send.at[d], plane_recv.at[q], plane_peer(q)).wait_recv()
+        remote(
+            part.at[owned(q)], r_plane.at[q], plane_send.at[d], plane_recv.at[q], plane_peer(q)
+        ).wait_recv()
         total = total + r_plane[q].astype(F32)
-    a32[0:used] = total
-    a16[...] = a32[...].astype(BF16)
-
-    out_z = []
+    a32[...] = total
+    a16[...] = total.astype(BF16)
+
+    def owns(q):
+        return q * zt < used
+
+    def tiles_of(q):
+        return pl.ds(core * HALF + plane * used + q * zt, zt)
+
     for d in range(1, nz):
         q = (z + d) % nz
-        out_z.append(
-            remote(a16.at[pl.ds(q * zt, zt)], r_z.at[z], z_send.at[d], z_recv.at[z], z_peer(q))
-        )
-    for copy in out_z:
-        copy.start()
-    total = a32[pl.ds(z * zt, zt)]
+
+        @pl.when(owns(q))
+        def _():
+            remote(
+                a16.at[pl.ds(q * zt, zt)], r_z.at[z], z_send.at[d], z_recv.at[z], z_peer(q)
+            ).start()
+
+    @pl.when(owns(z))
+    def _():
+        total = a32[pl.ds(z * zt, zt)]
+        for d in range(1, nz):
+            q = (z + nz - d) % nz
+            remote(a16.at[pl.ds(0, zt)], r_z.at[q], z_send.at[d], z_recv.at[q], z_peer(q)).wait_recv()
+            total = total + r_z[q].astype(F32)
+        full[tiles_of(z)] = total.astype(BF16)
+        own = full.at[tiles_of(z)]
+        for d in range(1, nz):
+            q = (z + d) % nz
+            remote(own, own, zg_send.at[d], zg_recv.at[z], z_peer(q)).start()
+
     for d in range(1, nz):
         q = (z + nz - d) % nz
-        remote(a16.at[pl.ds(0, zt)], r_z.at[q], z_send.at[d], z_recv.at[q], z_peer(q)).wait_recv()
-        total = total + r_z[q].astype(F32)
-    full[core, plane, pl.ds(z * zt, zt)] = total.astype(BF16)
-
-    mine = full.at[core, plane]
-    out_zg = []
-    for d in range(1, nz):
-        q = (z + d) % nz
-        own = mine.at[pl.ds(z * zt, zt)]
-        out_zg.append(remote(own, own, zg_send.at[d], zg_recv.at[z], z_peer(q)))
-    for copy in out_zg:
-        copy.start()
-    for d in range(1, nz):
-        q = (z + nz - d) % nz
-        theirs = mine.at[pl.ds(q * zt, zt)]
-        remote(theirs, theirs, zg_send.at[d], zg_recv.at[q], z_peer(q)).wait_recv()
+
+        @pl.when(owns(q))
+        def _():
+            theirs = full.at[tiles_of(q)]
+            remote(theirs, theirs, zg_send.at[d], zg_recv.at[q], z_peer(q)).wait_recv()
+
+    def gathered_at(half, q):
+        return full.at[pl.ds(half * HALF + q * used, used)]
 
     out_pg = []
     for d in range(1, n_plane):
         q = (plane + d) % n_plane
-        own = full.at[core, plane]
+        own = gathered_at(core, plane)
         out_pg.append(remote(own, own, pg_send.at[d], pg_recv.at[plane], plane_peer(q)))
     for copy in out_pg:
         copy.start()
     for d in range(1, n_plane):
         q = (plane + n_plane - d) % n_plane
-        theirs = full.at[core, q]
+        theirs = gathered_at(core, q)
         remote(theirs, theirs, pg_send.at[d], pg_recv.at[q], plane_peer(q)).wait_recv()
 
-    give = remote(full.at[core], full.at[core], cg_send.at[0], cg_recv.at[0], sibling)
+    mine, other = full.at[pl.ds(core * HALF, HALF)], full.at[pl.ds((1 - core) * HALF, HALF)]
+    give = remote(mine, mine, cg_send.at[0], cg_recv.at[0], sibling)
     give.start()
-    keep = pltpu.make_async_copy(full.at[core], grad_hbm.at[core], local_sem.at[3])
-    keep.start()
-    remote(full.at[1 - core], full.at[1 - core], cg_send.at[0], cg_recv.at[0], sibling).wait_recv()
-    take = pltpu.make_async_copy(full.at[1 - core], grad_hbm.at[1 - core], local_sem.at[4])
-    take.start()
-
-    for copy in halos + stats + [swap] + out_plane + out_z + out_zg + out_pg + [give]:
+    remote(other, other, cg_send.at[0], cg_recv.at[0], sibling).wait_recv()
+    keeps = []
+    for dy in range(3):
+        for k in range(3):
+            keeps.append(
+                pltpu.make_async_copy(
+                    full.at[pl.ds((dy * 3 + k) * 24, 24)],
+                    grad_hbm.at[pl.ds((k * 3 + dy) * 24, 24)],
+                    keep_sem.at[dy * 3 + k],
+                )
+            )
+    for copy in keeps:
+        copy.start()
+
+    for copy in halos + stats + [swap] + out_plane + out_pg + [give]:
         copy.wait_send()
-    keep.wait()
-    take.wait()
+    for d in range(1, nz):
+        q = (z + d) % nz
+
+        @pl.when(owns(q))
+        def _():
+            remote(
+                a16.at[pl.ds(q * zt, zt)], r_z.at[z], z_send.at[d], z_recv.at[z], z_peer(q)
+            ).wait_send()
+
+    @pl.when(owns(z))
+    def _():
+        own = full.at[tiles_of(z)]
+        for d in range(1, nz):
+            q = (z + d) % nz
+            remote(own, own, zg_send.at[d], zg_recv.at[z], z_peer(q)).wait_send()
+
+    for copy in keeps:
+        copy.wait()
 
 
 def per_device(nx, nz, ny, video, clip_first, kernel, bias, cotangent):
     _, frames, height, width, chans = video.shape
     half_h, half_w = height // 2, width // 2
     n_plane, n_tm = nx * ny, nx * nz
-    used = -(-TILES // n_plane)
+    used = HALF // n_plane
     zt = -(-used // nz)
-    slots = zt * nz
     any_space = pl.BlockSpec(memory_space=pl.ANY)
     vmem = pl.BlockSpec(memory_space=pltpu.VMEM)
-    smem = pl.BlockSpec(memory_space=pltpu.SMEM)
     sem = pltpu.SemaphoreType.DMA
     down, grad = pl.pallas_call(
         functools.partial(fused, nx, nz, ny),
         out_shape=(
             jax.ShapeDtypeStruct(cotangent.shape, BF16),
-            jax.ShapeDtypeStruct((2, n_plane, slots, 16, chans), BF16),
+            jax.ShapeDtypeStruct((27 * 8, 16, chans), BF16),
         ),
-        in_specs=[smem, vmem, any_space, any_space, any_space],
+        in_specs=[any_space] * 5,
         out_specs=(vmem, any_space),
         scratch_shapes=[
+            pltpu.SMEM(clip_first.shape, jnp.int32),
+            pltpu.VMEM((1, chans), F32),
             pltpu.VMEM((frames, height, width, chans), BF16),
             pltpu.VMEM((frames, height, width, chans), BF16),
             pltpu.VMEM((3, 3, 3, chans, chans), BF16),
@@ -387,15 +434,16 @@
             pltpu.VMEM((frames * chans, height * width), BF16),
             pltpu.VMEM((chans, height * width), BF16),
             pltpu.VMEM((n_tm, 8, chans), F32),
-            pltpu.VMEM((2, n_plane, slots, 16, chans), BF16),
+            pltpu.VMEM((2 * HALF, 16, chans), BF16),
+            pltpu.VMEM((HALF, 16, chans), BF16),
+            pltpu.VMEM((HALF, 16, chans), BF16),
             pltpu.VMEM((n_plane, used, 16, chans), BF16),
-            pltpu.VMEM((n_plane, used, 16, chans), BF16),
-            pltpu.VMEM((n_plane, used, 16, chans), BF16),
-            pltpu.VMEM((slots, 16, chans), F32),
-            pltpu.VMEM((slots, 16, chans), BF16),
+            pltpu.VMEM((used, 16, chans), F32),
+            pltpu.VMEM((used, 16, chans), BF16),
             pltpu.VMEM((nz, zt, 16, chans), BF16),
-            pltpu.VMEM((2, n_plane, slots, 16, chans), BF16),
+            pltpu.VMEM((2 * HALF, 16, chans), BF16),
             sem((5,)),
+            sem((9,)),
             sem((2,)),
             sem((2,)),
             sem((n_tm,)),
@@ -414,11 +462,9 @@
             sem((1,)),
         ],
         compiler_params=pltpu.CompilerParams(
-            collective_id=0, has_side_effects=True, vmem_limit_bytes=48 * 1024 * 1024
+            collective_id=0, has_side_effects=True, vmem_limit_bytes=62 * 1024 * 1024
         ),
     )(clip_first, bias.reshape(1, chans), video, kernel, cotangent)
-    grad = grad[:, :, :used].reshape(2, n_plane * used, 16, chans)[:, :TILES]
-    grad = grad.reshape(2, 27, chans // 2, chans).transpose(1, 0, 2, 3)
     return down, grad.reshape(3, 3, 3, chans, chans).astype(F32)
 
 

time: 70.8 us -> 67 us (0.946)
  local copies, waits for them, and re-layouts: 6.8 us -> 0.66 us
  other arithmetic: 0.19 us -> 2.62 us
    unnamed x11 -> x3, local copies, waits for them, and re-layouts: 5.07 us -> 0.66 us
    convert_element_type x1, other arithmetic: 0.19 us -> 2.62 us  [per_device(): return (down, grad.reshape(3, 3, 3, chans, chans).astype(F32))]
    convert_element_type x1 -> x0, local copies, waits for them, and re-layouts: 1.42 us -> none  [per_device(): return (down, grad.reshape(3, 3, 3, chans, chans).astype(F32))]
where the time goes in v2:
time: 67 us; the launch traced here: 66.9 us
  Pallas kernels  62.9 us (94%)
  other arithmetic  2.62 us (4%)
    pallas_call x1, Pallas kernels, per_device(): pl.pallas_call(functools.partial(fused, nx, nz, ny), out_shape=(jax.Shape...  62.9 us
    convert_element_type x1, other arithmetic, per_device(): return (down, grad.reshape(3, 3, 3, chans, chans).astype(F32))  2.62 us

profile of v2, /device:TPU:1, one launch (start us, length us, event | category | flops | bytes accessed | tf_op | source)
XLA Modules:
  0.0 66.9 jit_solution(12994122145429137171)
XLA Ops:
  0.6 62.9 %shard_map.68 = (bf16[1,2,8,32,128]{4,3,2,1,0:T(8,128)(2,1)}, bf16[216,16,128]{2,1,0:T(8,128)(2,1)}) custom-call(s32[1,2]{1,0:T(1,128)} %first_hbm.1, f32[1,128]{1,0:T(1,128)} %bitcast.4, bf16[1,2,16,64,128]{4,3,2,1,0:T(8,128)(2,1)} %video_hbm.1, bf16[3,3,3,128,128]{4,3,2,1,0:T(8,128)(2,1)} %kern_hbm.1, bf16[1,2,8,32,128]{4,3,2,1,0:T(8,128)(2,1)} %cot_hbm.1), custom_call_target="tpu_custom_call" | custom-call | tf_op jit(solution)/shard_map/pallas_call | solution.py:415
  63.6 0.0 copy-start
  63.6 2.6 %convert.1 = f32[3,3,3,128,128]{4,3,2,1,0:T(8,128)} convert(bf16[3,3,3,128,128]{4,3,2,1,0:T(8,128)(2,1)} %bitcast.3) | non-fusion elementwise | flops 442368 | bytes 2654208 | tf_op jit(solution)/shard_map/convert_element_type | solution.py:468
  66.2 0.0 copy-done
  66.2 0.7 copy.8
Async XLA Ops:
  63.6 2.6 %copy-start = (bf16[1,2,8,32,128]{4,3,2,1,0:T(8,128)(2,1)S(1)}, bf16[1,2,8,32,128]{4,3,2,1,0:T(8,128)(2,1)}, u32[]{:S(2)}) copy-start(bf16[1,2,8,32,128]{4,3,2,1,0:T(8,128)(2,1)} %get-tuple-element.8) | copy-start | bytes 393220

commit v3 on v1

v3 whole, which is shorter than its diff:
```python
import functools

import jax
import jax.numpy as jnp
from jax import lax
from jax.experimental import pallas as pl
from jax.experimental.pallas import tpu as pltpu
from jax.sharding import PartitionSpec as P

F32 = jnp.float32
BF16 = jnp.bfloat16
HALF = 28 * 4
CHUNK = 9 * 4


def fused(
    nx,
    nz,
    ny,
    sa,
    sb,
    first_hbm,
    bias_hbm,
    video_hbm,
    kern_hbm,
    cot_hbm,
    down_hbm,
    grad_hbm,
    first_ref,
    bias_ref,
    vid,
    halo,
    kern,
    cot,
    xs,
    acc,
    spread,
    pool,
    down,
    dts,
    gath,
    grads,
    r_pair,
    part,
    r1a,
    r1b,
    s1a,
    s1b,
    r2a,
    r2b,
    s2a,
    s2b,
    r3a,
    r3b,
    full,
    local_sem,
    near_send,
    near_recv,
    stat_send,
    stat_recv,
    pair_send,
    pair_recv,
    a1_send,
    a1_recv,
    b1_send,
    b1_recv,
    a2_send,
    a2_recv,
    b2_send,
    b2_recv,
    a3_send,
    a3_recv,
    b3_send,
    b3_recv,
    a4_send,
    a4_recv,
    b4_send,
    b4_recv,
    a5_send,
    a5_recv,
    b5_send,
    b5_recv,
    a6_send,
    a6_recv,
    b6_send,
    b6_recv,
):
    _, frames, height, width, chans = video_hbm.shape
    half_h, half_w = height // 2, width // 2
    pixels = height * width
    n_tm = nx * nz
    n_a = nx * ny * sa

    tm = lax.axis_index("tm")
    dp = lax.axis_index("dp")
    x, z = tm // nz, tm % nz
    y, core = dp // 2, dp % 2

    def at(tm_to, dp_to):
        return {"tm": tm_to, "dp": dp_to}

    def x_peer(q):
        return at(q * nz + z, dp)

    def y_peer(q):
        return at(tm, q * 2 + core)

    def z_peer(q):
        return at(x * nz + q, dp)

    sibling = at(tm, y * 2 + 1 - core)
    right = at((tm + 1) % n_tm, dp)
    left = at((tm + n_tm - 1) % n_tm, dp)

    def remote(src, dst, send, recv, to):
        return pltpu.make_async_remote_copy(
            src_ref=src,
            dst_ref=dst,
            send_sem=send,
            recv_sem=recv,
            device_id=to,
            device_id_type=pl.DeviceIdType.MESH,
        )

    loads = [
        pltpu.make_async_copy(video_hbm.at[0], vid, local_sem.at[0]),
        pltpu.make_async_copy(first_hbm, first_ref, local_sem.at[1]),
        pltpu.make_async_copy(cot_hbm.at[0, 1], cot.at[0], local_sem.at[2]),
        pltpu.make_async_copy(bias_hbm, bias_ref, local_sem.at[3]),
        pltpu.make_async_copy(kern_hbm, kern, local_sem.at[4]),
    ]
    for load in loads:
        load.start()

    barrier = pltpu.get_barrier_semaphore()
    peers = [at((tm + d) % n_tm, dp) for d in range(1, n_tm)]
    peers += [y_peer((y + d) % ny) for d in range(1, ny)]
    peers += [sibling]
    for peer in peers:
        pl.semaphore_signal(barrier, inc=1, device_id=peer, device_id_type=pl.DeviceIdType.MESH)

    loads[0].wait()
    loads[1].wait()
    rows = []
    for f in range(frames):
        value = vid[f].astype(F32)
        rows.append(jnp.sum(jnp.sum(value, axis=0), axis=0, keepdims=True))
        rows.append(jnp.sum(jnp.sum(value * value, axis=0), axis=0, keepdims=True))
    rows.append(jnp.zeros((4, chans), F32))
    stat = jnp.concatenate(rows, axis=0)
    lane8 = lax.broadcasted_iota(jnp.int32, (8, chans), 1)
    stat = stat + jnp.where(lane8 % 2 == 0, pltpu.roll(stat, chans - 1, 1), pltpu.roll(stat, 1, 1))
    stat = stat + jnp.where(lane8 % 4 < 2, pltpu.roll(stat, chans - 2, 1), pltpu.roll(stat, 2, 1))
    lane = lax.broadcasted_iota(jnp.int32, (1, chans), 1)
    low = jnp.where(lane % 2 == 0, stat[0:1], stat[1:2])
    high = jnp.where(lane % 2 == 0, stat[2:3], stat[3:4])
    first0 = jnp.full((1, chans), first_ref[0, 0], jnp.int32)
    first1 = jnp.full((1, chans), first_ref[0, 1], jnp.int32)
    gath[tm, 0:1] = jnp.where(lane % 4 < 2, low, high)
    gath[tm, 1:2] = first0.astype(F32)

    pl.semaphore_wait(barrier, len(peers))

    near = [
        remote(video_hbm.at[0, 1], halo.at[0], near_send.at[0], near_recv.at[0], right),
        remote(video_hbm.at[0, 0], halo.at[1], near_send.at[1], near_recv.at[1], left),
        remote(cot_hbm.at[0, 0], cot.at[1], near_send.at[2], near_recv.at[2], left),
    ]
    for d in range(1, n_tm):
        remote(gath.at[tm], gath.at[tm], stat_send.at[0], stat_recv.at[0], at((tm + d) % n_tm, dp)).start()
    for copy in near:
        copy.start()

    rim = jnp.zeros((width, 3 * chans), BF16)
    for s in range(4):
        xs[s, 0] = rim
        xs[s, height + 1] = rim
    for h in range(2):
        for j in range(27 * 4, HALF):
            grads[h * HALF + j] = jnp.zeros((16, chans), BF16)

    def widen(f):
        for i in range(half_h):
            quarter = cot[f, i].astype(F32) * 0.25
            spread[f * half_h + i, pl.ds(0, half_w, stride=2), :] = quarter
            spread[f * half_h + i, pl.ds(1, half_w, stride=2), :] = quarter

    loads[2].wait()
    widen(0)
    loads[3].wait()
    loads[4].wait()

    others = gath.at[pl.ds(0, n_tm - 1)]
    remote(others, others, stat_send.at[0], stat_recv.at[0], right).wait_recv()

    t0 = tm * frames
    t2 = (t0 + 2) % (n_tm * frames)
    first2 = gath[(tm + 1) % n_tm, 1:2].astype(jnp.int32)
    gathered = gath[...]
    frame = lax.broadcasted_iota(jnp.int32, gathered.shape, 0) * frames
    frame = frame + lax.broadcasted_iota(jnp.int32, gathered.shape, 2) % 4 // 2

    def moments(first, last):
        chosen = jnp.where((frame >= first[None]) & (frame <= last), gathered, 0.0)
        total = jnp.sum(chosen, axis=0)[0:1]
        count = jnp.maximum((last + 1 - first) * (pixels * 4), 1).astype(F32)
        total = total + jnp.where(lane % 4 < 2, pltpu.roll(total, chans - 2, 1), pltpu.roll(total, 2, 1))
        mean = jnp.where(lane % 2 == 0, total, pltpu.roll(total, 1, 1)) / count
        var = jnp.where(lane % 2 == 1, total, pltpu.roll(total, chans - 1, 1)) / count - mean * mean
        return mean, lax.rsqrt(var + 1e-05)

    col = lax.broadcasted_iota(jnp.int32, (width, chans), 0)

    def place(source, f, slot, mean, scale, keep):
        for r in range(height):
            value = (source[f, r].astype(F32) - mean) * scale
            if keep is not None:
                value = jnp.where(keep, value, 0.0)
            before = jnp.where(col == 0, 0.0, pltpu.roll(value, 1, 0))
            after = jnp.where(col == width - 1, 0.0, pltpu.roll(value, width - 1, 0))
            xs[slot, r + 1, :, 0:chans] = before.astype(BF16)
            xs[slot, r + 1, :, chans : 2 * chans] = value.astype(BF16)
            xs[slot, r + 1, :, 2 * chans : 3 * chans] = after.astype(BF16)

    def flag(condition):
        return jnp.where(condition, 1.0, 0.0)

    t0_t1 = flag(first1 <= t0)
    t0_t2 = flag(first2 <= t2 - 2)
    t1_t2 = flag(first2 <= t2 - 1)
    block = min(8, height)

    def patches(slot, r):
        parts = [xs[slot, r + dy : r + dy + block].reshape(block * width, 3 * chans) for dy in range(3)]
        return jnp.concatenate(parts, axis=1)

    def taps(k):
        return kern[k].reshape(9 * chans, chans)

    def dot(a, b):
        return jnp.dot(a, b, preferred_element_type=F32)

    place(vid, 0, 1, *moments(first0, t0), None)
    place(vid, 1, 2, *moments(first1, t0 + 1), None)
    for r in range(0, height, block):
        px = pl.ds(r * width, block * width)
        one = dot(patches(1, r), jnp.concatenate([taps(1), taps(0)], axis=1))
        two = dot(patches(2, r), jnp.concatenate([taps(2), taps(1)], axis=1))
        acc[0, px] = one[:, :chans] * t0_t1 + two[:, :chans]
        acc[1, px] = one[:, chans:] * t0_t2 + two[:, chans:] * t1_t2

    bias = bias_ref[...]

    def finish_conv(f, slot, k):
        for r in range(0, height, block):
            last = dot(patches(slot, r), taps(k))
            for m in range(block // 2):
                i = r // 2 + m
                px = slice(i * 2 * width, (i + 1) * 2 * width)
                value = acc[f, px] + last[m * 2 * width : (m + 1) * 2 * width] + bias
                logistic = 1.0 / (1.0 + jnp.exp(-value))
                active = value * logistic
                pool[f * half_h + i] = active[:width] + active[width:]
                slope = logistic * (1.0 + value * (1.0 - logistic))
                over = spread[f * half_h + i]
                dconv = jnp.concatenate([over, over], axis=0) * slope
                dts[f * chans : (f + 1) * chans, px] = dconv.T.astype(BF16)
        for i in range(half_h):
            even = pool[f * half_h + i, pl.ds(0, half_w, stride=2), :]
            odd = pool[f * half_h + i, pl.ds(1, half_w, stride=2), :]
            down[f, i] = ((even + odd) * 0.25).astype(BF16)

    near[0].wait_recv()
    place(halo, 0, 0, *moments(first1, t0 - 1), first1 <= t0 - 1)
    finish_conv(0, 0, 0)
    near[2].wait_recv()
    widen(1)
    near[1].wait_recv()
    place(halo, 1, 3, *moments(first2, t2), None)
    finish_conv(1, 3, 2)
    out_far = remote(down.at[1], down_hbm.at[0, 0], near_send.at[3], near_recv.at[3], right)
    out_near = pltpu.make_async_copy(down.at[0], down_hbm.at[0, 1], local_sem.at[5])
    out_far.start()
    out_near.start()

    sends = near + [out_far]

    def pair(c):
        tiles = pl.ds(c * CHUNK, CHUNK if c < 2 else HALF - 2 * CHUNK)
        src = grads.at[pl.ds((1 - core) * HALF + tiles.start, tiles.size)]
        return remote(src, r_pair.at[tiles], pair_send.at[c], pair_recv.at[c], sibling)

    def join_pair(c):
        pair(c).wait_recv()
        tiles = pl.ds(c * CHUNK, CHUNK if c < 2 else HALF - 2 * CHUNK)
        own = grads[pl.ds(core * HALF + tiles.start, tiles.size)].astype(F32)
        part[tiles] = (own + r_pair[tiles].astype(F32)).astype(BF16)

    def first_a(q):
        src = part.at[pl.ds(q * nx * sa, nx * sa)]
        return remote(src, r1a.at[y], a1_send.at[q], a1_recv.at[y], y_peer(q))

    def first_b(q):
        src = part.at[pl.ds(n_a + q * ny * sb, ny * sb)]
        return remote(src, r1b.at[x], b1_send.at[q], b1_recv.at[x], x_peer(q))

    def go(make, me, owners):
        for q in owners:

            @pl.when(q != me)
            def _():
                make(q).start()

    def a_ready(done):
        return [q for q in range(ny) if (q + 1) * nx * sa <= done]

    started = []
    for dy in range(3):
        shifted = [xs[s, dy : dy + height].reshape(pixels, 3 * chans) for s in range(4)]
        both = dts[...]
        r0 = dot(both[:chans], shifted[0])
        r1 = dot(both, shifted[1])
        r2 = dot(both, shifted[2])
        r3 = dot(both[chans:], shifted[3])
        m01, m02, m12 = t0_t1[:, 0:1], t0_t2[:, 0:1], t1_t2[:, 0:1]
        sums = [r0 + r1[chans:] * m02, r1[:chans] * m01 + r2[chans:] * m12, r2[:chans] + r3]
        for k in range(3):
            for dx in range(3):
                tile = sums[k][:, dx * chans : (dx + 1) * chans].T.astype(BF16)
                spot = ((dy * 3 + k) * 3 + dx) * 4
                for h in range(2):
                    for q in range(4):
                        start = (h * 4 + q) * 16
                        grads[h * HALF + spot + q] = tile[start : start + 16]
        sends.append(pair(dy))
        sends[-1].start()
        if dy > 0:
            join_pair(dy - 1)
            ready = [q for q in a_ready(dy * CHUNK) if q not in started]
            go(first_a, y, ready)
            started += ready
    join_pair(2)
    go(first_a, y, [q for q in range(ny) if q not in started])
    go(first_b, x, range(nx))

    def exchange(n, me, src_of, dst, send, recv, peer):
        copies = []
        for d in range(1, n):
            q = (me + d) % n
            copies.append(remote(src_of(q), dst.at[me], send.at[d], recv.at[me], peer(q)))
        return copies

    def arrived(n, me, dst, send, recv, peer):
        for d in range(1, n):
            q = (me + n - d) % n
            remote(dst.at[q], dst.at[q], send.at[d], recv.at[q], peer(q)).wait_recv()

    def summed(n, me, own, dst):
        total = own.astype(F32)
        for d in range(1, n):
            total = total + dst[(me + n - d) % n].astype(F32)
        return total.astype(BF16)

    arrived(ny, y, r1a, a1_send, a1_recv, y_peer)
    s1a[...] = summed(ny, y, part[pl.ds(y * nx * sa, nx * sa)], r1a)
    copies = exchange(nx, x, lambda q: s1a.at[pl.ds(q * sa, sa)], r2a, a2_send, a2_recv, x_peer)
    arrived_b = functools.partial(arrived, nx, x, r1b, b1_send, b1_recv, x_peer)
    for copy in copies:
        copy.start()
    sends += copies
    arrived_b()
    s1b[...] = summed(nx, x, part[pl.ds(n_a + x * ny * sb, ny * sb)], r1b)
    copies = exchange(ny, y, lambda q: s1b.at[pl.ds(q * sb, sb)], r2b, b2_send, b2_recv, y_peer)
    for copy in copies:
        copy.start()
    sends += copies

    arrived(nx, x, r2a, a2_send, a2_recv, x_peer)
    s2a[...] = summed(nx, x, s1a[pl.ds(x * sa, sa)], r2a)
    copies = exchange(nz, z, lambda q: s2a, r3a, a3_send, a3_recv, z_peer)
    for copy in copies:
        copy.start()
    sends += copies
    arrived(ny, y, r2b, b2_send, b2_recv, y_peer)
    s2b[...] = summed(ny, y, s1b[pl.ds(y * sb, sb)], r2b)
    copies = exchange(nz, z, lambda q: s2b, r3b, b3_send, b3_recv, z_peer)
    for copy in copies:
        copy.start()
    sends += copies

    base = core * HALF

    def a_line(q):
        return full.at[pl.ds(base + q * nx * sa, nx * sa)]

    def b_line(q):
        return full.at[pl.ds(base + n_a + q * ny * sb, ny * sb)]

    def a_piece(q):
        return full.at[pl.ds(base + (y * nx + q) * sa, sa)]

    def b_piece(q):
        return full.at[pl.ds(base + n_a + (x * ny + q) * sb, sb)]

    def spread_out(n, me, piece, send, recv, peer):
        copies = []
        for d in range(1, n):
            q = (me + d) % n
            copies.append(remote(piece(me), piece(me), send.at[d], recv.at[me], peer(q)))
            copies[-1].start()
        return copies

    def collected(n, me, piece, send, recv, peer, then=None):
        for d in range(1, n):
            q = (me + n - d) % n
            remote(piece(q), piece(q), send.at[d], recv.at[q], peer(q)).wait_recv()
            if then is not None:
                then(q)

    arrived(nz, z, r3a, a3_send, a3_recv, z_peer)
    full[pl.ds(base + (y * nx + x) * sa, sa)] = summed(nz, z, s2a[...], r3a)
    sends += spread_out(nx, x, a_piece, a4_send, a4_recv, x_peer)
    arrived(nz, z, r3b, b3_send, b3_recv, z_peer)
    full[pl.ds(base + n_a + (x * ny + y) * sb, sb)] = summed(nz, z, s2b[...], r3b)
    sends += spread_out(ny, y, b_piece, b4_send, b4_recv, y_peer)

    def give_a(q):
        sends.append(remote(a_line(q), a_line(q), a6_send.at[q], a6_recv.at[q], sibling))
        sends[-1].start()

    def give_b(q):
        sends.append(remote(b_line(q), b_line(q), b6_send.at[q], b6_recv.at[q], sibling))
        sends[-1].start()

    collected(nx, x, a_piece, a4_send, a4_recv, x_peer)
    sends += spread_out(ny, y, a_line, a5_send, a5_recv, y_peer)
    give_a(y)
    collected(ny, y, b_piece, b4_send, b4_recv, y_peer)
    sends += spread_out(nx, x, b_line, b5_send, b5_recv, x_peer)
    give_b(x)
    collected(ny, y, a_line, a5_send, a5_recv, y_peer, give_a)
    collected(nx, x, b_line, b5_send, b5_recv, x_peer, give_b)
    mine = pltpu.make_async_copy(
        full.at[pl.ds(base, HALF)], grad_hbm.at[pl.ds(base, HALF)], local_sem.at[6]
    )
    mine.start()
    base = (1 - core) * HALF
    for q in range(ny):
        remote(a_line(q), a_line(q), a6_send.at[q], a6_recv.at[q], sibling).wait_recv()
    for q in range(nx):
        remote(b_line(q), b_line(q), b6_send.at[q], b6_recv.at[q], sibling).wait_recv()
    theirs = pltpu.make_async_copy(
        full.at[pl.ds(base, HALF)], grad_hbm.at[pl.ds(base, HALF)], local_sem.at[7]
    )
    theirs.start()

    remote(others, others, stat_send.at[0], stat_recv.at[0], right).wait_send()
    for copy in sends:
        copy.wait_send()
    for make, me, n in ((first_a, y, ny), (first_b, x, nx)):
        for q in range(n):

            @pl.when(q != me)
            def _():
                make(q).wait_send()

    out_far.wait_recv()
    out_near.wait()
    mine.wait()
    theirs.wait()


def widen_result(grad_hbm, down_hbm, grad_out, down_out, tiles, wide, sems):
    pass_on = pltpu.make_async_copy(down_hbm, down_out, sems.at[0])
    loads = []
    for dy in range(3):
        for h in range(2):
            span = pl.ds(h * HALF + dy * CHUNK, CHUNK)
            loads.append(pltpu.make_async_copy(grad_hbm.at[span], tiles.at[span], sems.at[1 + dy * 2 + h]))
    for load in loads:
        load.start()
    pass_on.start()
    stores = []
    for dy in range(3):
        for h in range(2):
            loads[dy * 2 + h].wait()
        for k in range(3):
            tap = k * 9 + dy * 3
            for dx in range(3):
                for h in range(2):
                    for q in range(4):
                        spot = h * HALF + ((dy * 3 + k) * 3 + dx) * 4 + q
                        start = (h * 4 + q) * 16
                        wide[tap + dx, start : start + 16] = tiles[spot].astype(F32)
            group = pl.ds(tap, 3)
            stores.append(pltpu.make_async_copy(wide.at[group], grad_out.at[group], sems.at[7 + dy * 3 + k]))
            stores[-1].start()
    for store in stores:
        store.wait()
    pass_on.wait()


def per_device(nx, nz, ny, video, clip_first, kernel, bias, cotangent):
    _, frames, height, width, chans = video.shape
    half_h, half_w = height // 2, width // 2
    n_tm = nx * nz
    owned = HALF // (nx * ny)
    sa, sb = owned - owned // 2, owned // 2
    any_space = pl.BlockSpec(memory_space=pl.ANY)
    sem = pltpu.SemaphoreType.DMA

    def tiles(*shape):
        return pltpu.VMEM((*shape, 16, chans), BF16)

    def both(n):
        return [sem((n,)), sem((n,))]

    down, grad = pl.pallas_call(
        functools.partial(fused, nx, nz, ny, sa, sb),
        out_shape=(
            jax.ShapeDtypeStruct(cotangent.shape, BF16),
            jax.ShapeDtypeStruct((2 * HALF, 16, chans), BF16),
        ),
        in_specs=[any_space] * 5,
        out_specs=(any_space, any_space),
        scratch_shapes=[
            pltpu.SMEM(clip_first.shape, jnp.int32),
            pltpu.VMEM((1, chans), F32),
            pltpu.VMEM((frames, height, width, chans), BF16),
            pltpu.VMEM((frames, height, width, chans), BF16),
            pltpu.VMEM((3, 3, 3, chans, chans), BF16),
            pltpu.VMEM((frames, half_h, half_w, chans), BF16),
            pltpu.VMEM((4, height + 2, width, 3 * chans), BF16),
            pltpu.VMEM((frames, height * width, chans), F32),
            pltpu.VMEM((frames * half_h, width, chans), F32),
            pltpu.VMEM((frames * half_h, width, chans), F32),
            pltpu.VMEM((frames, half_h, half_w, chans), BF16),
            pltpu.VMEM((frames * chans, height * width), BF16),
            pltpu.VMEM((n_tm, 2, chans), F32),
            tiles(2 * HALF),
            tiles(HALF),
            tiles(HALF),
            tiles(ny, nx * sa),
            tiles(nx, ny * sb),
            tiles(nx * sa),
            tiles(ny * sb),
            tiles(nx, sa),
            tiles(ny, sb),
            tiles(sa),
            tiles(sb),
            tiles(nz, sa),
            tiles(nz, sb),
            tiles(2 * HALF),
            sem((8,)),
            *both(4),
            *both(1),
            *both(3),
            *both(ny),
            *both(nx),
            *both(nx),
            *both(ny),
            *both(nz),
            *both(nz),
            *both(nx),
            *both(ny),
            *both(ny),
            *both(nx),
            *both(ny),
            *both(nx),
        ],
        compiler_params=pltpu.CompilerParams(
            collective_id=0, has_side_effects=True, vmem_limit_bytes=62 * 1024 * 1024
        ),
    )(clip_first, bias.reshape(1, chans), video, kernel, cotangent)
    grad, down = pl.pallas_call(
        widen_result,
        out_shape=(
            jax.ShapeDtypeStruct((27, chans, chans), F32),
            jax.ShapeDtypeStruct(cotangent.shape, BF16),
        ),
        in_specs=[any_space] * 2,
        out_specs=(any_space, any_space),
        scratch_shapes=[
            tiles(2 * HALF),
            pltpu.VMEM((27, chans, chans), F32),
            sem((16,)),
        ],
        compiler_params=pltpu.CompilerParams(vmem_limit_bytes=62 * 1024 * 1024),
    )(grad, down)
    return down, grad.reshape(3, 3, 3, chans, chans)


def solution(mesh):
    n_tm, n_dp = mesh.shape["tm"], mesh.shape["dp"]
    nz = 8 if n_tm == 32 else 2
    in_specs = (
        P("dp", "tm", None, None, None),
        P("dp", "tm"),
        P(),
        P(),
        P("dp", "tm", None, None, None),
    )
    out_specs = (P("dp", "tm", None, None, None), P())
    return jax.shard_map(
        functools.partial(per_device, n_tm // nz, nz, n_dp // 2),
        mesh=mesh,
        in_specs=in_specs,
        out_specs=out_specs,
        check_vma=False,
    )
```

time: 70.8 us -> 59.6 us (0.84)
  local copies, waits for them, and re-layouts: 6.8 us -> 0 us
  Pallas kernels: 62.9 us -> 58.8 us
    unnamed x11 -> x0, local copies, waits for them, and re-layouts: 5.07 us -> none
    pallas_call x1 -> x2, Pallas kernels: 62.9 us -> 58.8 us  [the longest x1 53.6 us: per_device(): pl.pallas_call(functools.partial(fused, nx, nz, ny, sa, sb), out_shape=(j...]
    convert_element_type x1 -> x0, local copies, waits for them, and re-layouts: 1.42 us -> none  [per_device(): return (down, grad.reshape(3, 3, 3, chans, chans).astype(F32))]
where the time goes in v3:
time: 59.6 us; the launch traced here: 59.5 us
  Pallas kernels  58.8 us (99%)
  between operations  0.64 us (1%)
    pallas_call x1, Pallas kernels, per_device(): pl.pallas_call(functools.partial(fused, nx, nz, ny, sa, sb), out_shape=(j...  53.6 us
    pallas_call x1, Pallas kernels, per_device(): pl.pallas_call(widen_result, out_shape=(jax.ShapeDtypeStruct((27, chans,...  5.22 us

profile of v3, /device:TPU:1, one launch (start us, length us, event | category | flops | bytes accessed | tf_op | source)
XLA Modules:
  0.0 59.5 jit_solution(6098936215310078413)
XLA Ops:
  0.6 53.6 %shard_map.68 = (bf16[1,2,8,32,128]{4,3,2,1,0:T(8,128)(2,1)}, bf16[224,16,128]{2,1,0:T(8,128)(2,1)}) custom-call(s32[1,2]{1,0:T(1,128)} %first_hbm.1, f32[1,128]{1,0:T(1,128)} %bitcast.2, bf16[1,2,16,64,128]{4,3,2,1,0:T(8,128)(2,1)} %video_hbm.1, bf16[3,3,3,128,128]{4,3,2,1,0:T(8,128)(2,1)} %kern_hbm.1, bf16[1,2,8,32,128]{4,3,2,1,0:T(8,128)(2,1)} %cot_hbm.1), custom_call_target="tpu_custom_call" | custom-call | tf_op jit(solution)/shard_map/pallas_call | solution.py:518
  54.2 5.2 %shard_map.69 = (f32[27,128,128]{2,1,0:T(8,128)}, bf16[1,2,8,32,128]{4,3,2,1,0:T(8,128)(2,1)}) custom-call(bf16[224,16,128]{2,1,0:T(8,128)(2,1)} %get-tuple-element.6.grad_hbm, bf16[1,2,8,32,128]{4,3,2,1,0:T(8,128)(2,1)} %get-tuple-element.7.down_hbm), custom_call_target="tpu_custom_call" | custom-call | tf_op jit(solution)/shard_map/pallas_call | solution.py:575

commit v4 on v3

--- a/solution.py
+++ b/solution.py
@@ -54,36 +54,12 @@
     r3b,
     full,
     local_sem,
-    near_send,
+    sent,
     near_recv,
-    stat_send,
-    stat_recv,
-    pair_send,
     pair_recv,
-    a1_send,
-    a1_recv,
-    b1_send,
-    b1_recv,
-    a2_send,
-    a2_recv,
-    b2_send,
-    b2_recv,
-    a3_send,
-    a3_recv,
-    b3_send,
-    b3_recv,
-    a4_send,
-    a4_recv,
-    b4_send,
-    b4_recv,
-    a5_send,
-    a5_recv,
-    b5_send,
-    b5_recv,
-    a6_send,
-    a6_recv,
-    b6_send,
-    b6_recv,
+    stage,
+    line_a,
+    line_b,
 ):
     _, frames, height, width, chans = video_hbm.shape
     half_h, half_w = height // 2, width // 2
@@ -162,14 +138,15 @@
     pl.semaphore_wait(barrier, len(peers))
 
     near = [
-        remote(video_hbm.at[0, 1], halo.at[0], near_send.at[0], near_recv.at[0], right),
-        remote(video_hbm.at[0, 0], halo.at[1], near_send.at[1], near_recv.at[1], left),
-        remote(cot_hbm.at[0, 0], cot.at[1], near_send.at[2], near_recv.at[2], left),
+        remote(video_hbm.at[0, 1], halo.at[0], sent.at[0], near_recv.at[0], right),
+        remote(video_hbm.at[0, 0], halo.at[1], sent.at[0], near_recv.at[1], left),
+        remote(cot_hbm.at[0, 0], cot.at[1], sent.at[0], near_recv.at[2], left),
     ]
+    for copy in near[:2]:
+        copy.start()
     for d in range(1, n_tm):
-        remote(gath.at[tm], gath.at[tm], stat_send.at[0], stat_recv.at[0], at((tm + d) % n_tm, dp)).start()
-    for copy in near:
-        copy.start()
+        remote(gath.at[tm], gath.at[tm], sent.at[4], stage.at[0], at((tm + d) % n_tm, dp)).start()
+    near[2].start()
 
     rim = jnp.zeros((width, 3 * chans), BF16)
     for s in range(4):
@@ -191,7 +168,7 @@
     loads[4].wait()
 
     others = gath.at[pl.ds(0, n_tm - 1)]
-    remote(others, others, stat_send.at[0], stat_recv.at[0], right).wait_recv()
+    remote(others, others, sent.at[4], stage.at[0], right).wait_recv()
 
     t0 = tm * frames
     t2 = (t0 + 2) % (n_tm * frames)
@@ -278,17 +255,16 @@
     near[1].wait_recv()
     place(halo, 1, 3, *moments(first2, t2), None)
     finish_conv(1, 3, 2)
-    out_far = remote(down.at[1], down_hbm.at[0, 0], near_send.at[3], near_recv.at[3], right)
+    out_far = remote(down.at[1], down_hbm.at[0, 0], sent.at[0], near_recv.at[3], right)
     out_near = pltpu.make_async_copy(down.at[0], down_hbm.at[0, 1], local_sem.at[5])
     out_far.start()
     out_near.start()
 
-    sends = near + [out_far]
 
     def pair(c):
         tiles = pl.ds(c * CHUNK, CHUNK if c < 2 else HALF - 2 * CHUNK)
         src = grads.at[pl.ds((1 - core) * HALF + tiles.start, tiles.size)]
-        return remote(src, r_pair.at[tiles], pair_send.at[c], pair_recv.at[c], sibling)
+        return remote(src, r_pair.at[tiles], sent.at[1], pair_recv.at[c], sibling)
 
     def join_pair(c):
         pair(c).wait_recv()
@@ -298,11 +274,11 @@
 
     def first_a(q):
         src = part.at[pl.ds(q * nx * sa, nx * sa)]
-        return remote(src, r1a.at[y], a1_send.at[q], a1_recv.at[y], y_peer(q))
+        return remote(src, r1a.at[y], sent.at[1], stage.at[1], y_peer(q))
 
     def first_b(q):
         src = part.at[pl.ds(n_a + q * ny * sb, ny * sb)]
-        return remote(src, r1b.at[x], b1_send.at[q], b1_recv.at[x], x_peer(q))
+        return remote(src, r1b.at[x], sent.at[1], stage.at[2], x_peer(q))
 
     def go(make, me, owners):
         for q in owners:
@@ -332,8 +308,7 @@
                     for q in range(4):
                         start = (h * 4 + q) * 16
                         grads[h * HALF + spot + q] = tile[start : start + 16]
-        sends.append(pair(dy))
-        sends[-1].start()
+        pair(dy).start()
         if dy > 0:
             join_pair(dy - 1)
             ready = [q for q in a_ready(dy * CHUNK) if q not in started]
@@ -343,17 +318,14 @@
     go(first_a, y, [q for q in range(ny) if q not in started])
     go(first_b, x, range(nx))
 
-    def exchange(n, me, src_of, dst, send, recv, peer):
-        copies = []
+    def exchange(n, me, src_of, dst, place, peer):
         for d in range(1, n):
             q = (me + d) % n
-            copies.append(remote(src_of(q), dst.at[me], send.at[d], recv.at[me], peer(q)))
-        return copies
-
-    def arrived(n, me, dst, send, recv, peer):
-        for d in range(1, n):
-            q = (me + n - d) % n
-            remote(dst.at[q], dst.at[q], send.at[d], recv.at[q], peer(q)).wait_recv()
+            remote(src_of(q), dst.at[me], sent.at[2], stage.at[place], peer(q)).start()
+
+    def arrived(n, dst, place):
+        rows = dst.at[pl.ds(0, n - 1)]
+        remote(rows, rows, sent.at[2], stage.at[place], sibling).wait_recv()
 
     def summed(n, me, own, dst):
         total = own.astype(F32)
@@ -361,117 +333,94 @@
             total = total + dst[(me + n - d) % n].astype(F32)
         return total.astype(BF16)
 
-    arrived(ny, y, r1a, a1_send, a1_recv, y_peer)
+    arrived(ny, r1a, 1)
     s1a[...] = summed(ny, y, part[pl.ds(y * nx * sa, nx * sa)], r1a)
-    copies = exchange(nx, x, lambda q: s1a.at[pl.ds(q * sa, sa)], r2a, a2_send, a2_recv, x_peer)
-    arrived_b = functools.partial(arrived, nx, x, r1b, b1_send, b1_recv, x_peer)
-    for copy in copies:
+    exchange(nx, x, lambda q: s1a.at[pl.ds(q * sa, sa)], r2a, 3, x_peer)
+    arrived(nx, r1b, 2)
+    s1b[...] = summed(nx, x, part[pl.ds(n_a + x * ny * sb, ny * sb)], r1b)
+    exchange(ny, y, lambda q: s1b.at[pl.ds(q * sb, sb)], r2b, 4, y_peer)
+
+    arrived(nx, r2a, 3)
+    s2a[...] = summed(nx, x, s1a[pl.ds(x * sa, sa)], r2a)
+    exchange(nz, z, lambda q: s2a, r3a, 5, z_peer)
+    arrived(ny, r2b, 4)
+    s2b[...] = summed(ny, y, s1b[pl.ds(y * sb, sb)], r2b)
+    exchange(nz, z, lambda q: s2b, r3b, 6, z_peer)
+
+    base = core * HALF
+
+    def a_line(q, start=base):
+        return full.at[pl.ds(start + q * nx * sa, nx * sa)]
+
+    def b_line(q, start=base):
+        return full.at[pl.ds(start + n_a + q * ny * sb, ny * sb)]
+
+    def spread_out(n, me, piece, group, recv, peer):
+        for d in range(1, n):
+            remote(piece, piece, sent.at[group], recv, peer((me + d) % n)).start()
+
+    def some(tiles):
+        return full.at[pl.ds(0, tiles)]
+
+    arrived(nz, r3a, 5)
+    a_piece = full.at[pl.ds(base + (y * nx + x) * sa, sa)]
+    a_piece[...] = summed(nz, z, s2a[...], r3a)
+    spread_out(nx, x, a_piece, 2, stage.at[7], x_peer)
+    arrived(nz, r3b, 6)
+    b_piece = full.at[pl.ds(base + n_a + (x * ny + y) * sb, sb)]
+    b_piece[...] = summed(nz, z, s2b[...], r3b)
+    spread_out(ny, y, b_piece, 2, stage.at[8], y_peer)
+
+    def give_a(q):
+        remote(a_line(q), a_line(q), sent.at[3], stage.at[9], sibling).start()
+
+    def give_b(q):
+        remote(b_line(q), b_line(q), sent.at[3], stage.at[10], sibling).start()
+
+    remote(some((nx - 1) * sa), some((nx - 1) * sa), sent.at[2], stage.at[7], sibling).wait_recv()
+    spread_out(ny, y, a_line(y), 3, line_a.at[y], y_peer)
+    give_a(y)
+    remote(some((ny - 1) * sb), some((ny - 1) * sb), sent.at[2], stage.at[8], sibling).wait_recv()
+    spread_out(nx, x, b_line(x), 3, line_b.at[x], x_peer)
+    give_b(x)
+    for d in range(1, ny):
+        q = (y + ny - d) % ny
+        remote(a_line(q), a_line(q), sent.at[3], line_a.at[q], sibling).wait_recv()
+        give_a(q)
+    for d in range(1, nx):
+        q = (x + nx - d) % nx
+        remote(b_line(q), b_line(q), sent.at[3], line_b.at[q], sibling).wait_recv()
+        give_b(q)
+
+    def write(start, size, place):
+        tiles = pl.ds(start, size)
+        copy = pltpu.make_async_copy(full.at[tiles], grad_hbm.at[tiles], local_sem.at[place])
         copy.start()
-    sends += copies
-    arrived_b()
-    s1b[...] = summed(nx, x, part[pl.ds(n_a + x * ny * sb, ny * sb)], r1b)
-    copies = exchange(ny, y, lambda q: s1b.at[pl.ds(q * sb, sb)], r2b, b2_send, b2_recv, y_peer)
-    for copy in copies:
-        copy.start()
-    sends += copies
-
-    arrived(nx, x, r2a, a2_send, a2_recv, x_peer)
-    s2a[...] = summed(nx, x, s1a[pl.ds(x * sa, sa)], r2a)
-    copies = exchange(nz, z, lambda q: s2a, r3a, a3_send, a3_recv, z_peer)
-    for copy in copies:
-        copy.start()
-    sends += copies
-    arrived(ny, y, r2b, b2_send, b2_recv, y_peer)
-    s2b[...] = summed(ny, y, s1b[pl.ds(y * sb, sb)], r2b)
-    copies = exchange(nz, z, lambda q: s2b, r3b, b3_send, b3_recv, z_peer)
-    for copy in copies:
-        copy.start()
-    sends += copies
-
-    base = core * HALF
-
-    def a_line(q):
-        return full.at[pl.ds(base + q * nx * sa, nx * sa)]
-
-    def b_line(q):
-        return full.at[pl.ds(base + n_a + q * ny * sb, ny * sb)]
-
-    def a_piece(q):
-        return full.at[pl.ds(base + (y * nx + q) * sa, sa)]
-
-    def b_piece(q):
-        return full.at[pl.ds(base + n_a + (x * ny + q) * sb, sb)]
-
-    def spread_out(n, me, piece, send, recv, peer):
-        copies = []
-        for d in range(1, n):
-            q = (me + d) % n
-            copies.append(remote(piece(me), piece(me), send.at[d], recv.at[me], peer(q)))
-            copies[-1].start()
-        return copies
-
-    def collected(n, me, piece, send, recv, peer, then=None):
-        for d in range(1, n):
-            q = (me + n - d) % n
-            remote(piece(q), piece(q), send.at[d], recv.at[q], peer(q)).wait_recv()
-            if then is not None:
-                then(q)
-
-    arrived(nz, z, r3a, a3_send, a3_recv, z_peer)
-    full[pl.ds(base + (y * nx + x) * sa, sa)] = summed(nz, z, s2a[...], r3a)
-    sends += spread_out(nx, x, a_piece, a4_send, a4_recv, x_peer)
-    arrived(nz, z, r3b, b3_send, b3_recv, z_peer)
-    full[pl.ds(base + n_a + (x * ny + y) * sb, sb)] = summed(nz, z, s2b[...], r3b)
-    sends += spread_out(ny, y, b_piece, b4_send, b4_recv, y_peer)
-
-    def give_a(q):
-        sends.append(remote(a_line(q), a_line(q), a6_send.at[q], a6_recv.at[q], sibling))
-        sends[-1].start()
-
-    def give_b(q):
-        sends.append(remote(b_line(q), b_line(q), b6_send.at[q], b6_recv.at[q], sibling))
-        sends[-1].start()
-
-    collected(nx, x, a_piece, a4_send, a4_recv, x_peer)
-    sends += spread_out(ny, y, a_line, a5_send, a5_recv, y_peer)
-    give_a(y)
-    collected(ny, y, b_piece, b4_send, b4_recv, y_peer)
-    sends += spread_out(nx, x, b_line, b5_send, b5_recv, x_peer)
-    give_b(x)
-    collected(ny, y, a_line, a5_send, a5_recv, y_peer, give_a)
-    collected(nx, x, b_line, b5_send, b5_recv, x_peer, give_b)
-    mine = pltpu.make_async_copy(
-        full.at[pl.ds(base, HALF)], grad_hbm.at[pl.ds(base, HALF)], local_sem.at[6]
-    )
-    mine.start()
+        return copy
+
+    writes = [write(base, HALF, 6)]
     base = (1 - core) * HALF
-    for q in range(ny):
-        remote(a_line(q), a_line(q), a6_send.at[q], a6_recv.at[q], sibling).wait_recv()
-    for q in range(nx):
-        remote(b_line(q), b_line(q), b6_send.at[q], b6_recv.at[q], sibling).wait_recv()
-    theirs = pltpu.make_async_copy(
-        full.at[pl.ds(base, HALF)], grad_hbm.at[pl.ds(base, HALF)], local_sem.at[7]
-    )
-    theirs.start()
-
-    remote(others, others, stat_send.at[0], stat_recv.at[0], right).wait_send()
-    for copy in sends:
-        copy.wait_send()
-    for make, me, n in ((first_a, y, ny), (first_b, x, nx)):
-        for q in range(n):
-
-            @pl.when(q != me)
-            def _():
-                make(q).wait_send()
+    remote(some(n_a), some(n_a), sent.at[3], stage.at[9], sibling).wait_recv()
+    writes.append(write(base, n_a, 7))
+    remote(some(HALF - n_a), some(HALF - n_a), sent.at[3], stage.at[10], sibling).wait_recv()
+    writes.append(write(base + n_a, HALF - n_a, 8))
+
+    remote(others, others, sent.at[4], stage.at[0], right).wait_send()
+    lines = (ny - 1) * nx * sa + (nx - 1) * ny * sb
+    pieces = 2 * ((nx - 1) * sa + (ny - 1) * sb) + (nz - 1) * (sa + sb)
+    frames_out = frames * (pixels + half_h * half_w) // 16
+    for group, tiles in ((0, frames_out), (1, HALF + lines), (2, pieces), (3, HALF + lines)):
+        remote(some(tiles), some(tiles), sent.at[group], stage.at[0], sibling).wait_send()
 
     out_far.wait_recv()
     out_near.wait()
-    mine.wait()
-    theirs.wait()
-
-
-def widen_result(grad_hbm, down_hbm, grad_out, down_out, tiles, wide, sems):
-    pass_on = pltpu.make_async_copy(down_hbm, down_out, sems.at[0])
+    for copy in writes:
+        copy.wait()
+
+
+def widen_result(grad_hbm, down_hbm, grad_out, down_out, tiles, wide, down, sems):
+    take = pltpu.make_async_copy(down_hbm, down, sems.at[0])
+    pass_on = pltpu.make_async_copy(down, down_out, sems.at[0])
     loads = []
     for dy in range(3):
         for h in range(2):
@@ -479,7 +428,7 @@
             loads.append(pltpu.make_async_copy(grad_hbm.at[span], tiles.at[span], sems.at[1 + dy * 2 + h]))
     for load in loads:
         load.start()
-    pass_on.start()
+    take.start()
     stores = []
     for dy in range(3):
         for h in range(2):
@@ -495,6 +444,8 @@
             group = pl.ds(tap, 3)
             stores.append(pltpu.make_async_copy(wide.at[group], grad_out.at[group], sems.at[7 + dy * 3 + k]))
             stores[-1].start()
+    take.wait()
+    pass_on.start()
     for store in stores:
         store.wait()
     pass_on.wait()
@@ -511,9 +462,6 @@
 
     def tiles(*shape):
         return pltpu.VMEM((*shape, 16, chans), BF16)
-
-    def both(n):
-        return [sem((n,)), sem((n,))]
 
     down, grad = pl.pallas_call(
         functools.partial(fused, nx, nz, ny, sa, sb),
@@ -551,22 +499,13 @@
             tiles(nz, sa),
             tiles(nz, sb),
             tiles(2 * HALF),
-            sem((8,)),
-            *both(4),
-            *both(1),
-            *both(3),
-            *both(ny),
-            *both(nx),
-            *both(nx),
-            *both(ny),
-            *both(nz),
-            *both(nz),
-            *both(nx),
-            *both(ny),
-            *both(ny),
-            *both(nx),
-            *both(ny),
-            *both(nx),
+            sem((9,)),
+            sem((5,)),
+            sem((4,)),
+            sem((3,)),
+            sem((11,)),
+            sem((ny,)),
+            sem((nx,)),
         ],
         compiler_params=pltpu.CompilerParams(
             collective_id=0, has_side_effects=True, vmem_limit_bytes=62 * 1024 * 1024
@@ -583,6 +522,7 @@
         scratch_shapes=[
             tiles(2 * HALF),
             pltpu.VMEM((27, chans, chans), F32),
+            pltpu.VMEM(cotangent.shape, BF16),
             sem((16,)),
         ],
         compiler_params=pltpu.CompilerParams(vmem_limit_bytes=62 * 1024 * 1024),

time: 59.6 us -> 60 us (level)
    pallas_call x1, Pallas kernels: 53.6 us -> 56.8 us  [per_device(): pl.pallas_call(functools.partial(fused, nx, nz, ny, sa, sb), out_shape=(j...]
    pallas_call x1, Pallas kernels: 5.22 us -> 2.37 us  [per_device(): pl.pallas_call(widen_result, out_shape=(jax.ShapeDtypeStruct((27, chans,...]
where the time goes in v4:
time: 60 us; the launch traced here: 59.9 us
  Pallas kernels  59.2 us (99%)
  between operations  0.64 us (1%)
    pallas_call x1, Pallas kernels, per_device(): pl.pallas_call(functools.partial(fused, nx, nz, ny, sa, sb), out_shape=(j...  56.8 us
    pallas_call x1, Pallas kernels, per_device(): pl.pallas_call(widen_result, out_shape=(jax.ShapeDtypeStruct((27, chans,...  2.37 us

profile of v4, /device:TPU:1, one launch (start us, length us, event | category | flops | bytes accessed | tf_op | source)
XLA Modules:
  0.0 59.9 jit_solution(15401056983233951832)
XLA Ops:
  0.6 56.8 %shard_map.68 = (bf16[1,2,8,32,128]{4,3,2,1,0:T(8,128)(2,1)}, bf16[224,16,128]{2,1,0:T(8,128)(2,1)}) custom-call(s32[1,2]{1,0:T(1,128)} %first_hbm.1, f32[1,128]{1,0:T(1,128)} %bitcast.2, bf16[1,2,16,64,128]{4,3,2,1,0:T(8,128)(2,1)} %video_hbm.1, bf16[3,3,3,128,128]{4,3,2,1,0:T(8,128)(2,1)} %kern_hbm.1, bf16[1,2,8,32,128]{4,3,2,1,0:T(8,128)(2,1)} %cot_hbm.1), custom_call_target="tpu_custom_call" | custom-call | tf_op jit(solution)/shard_map/pallas_call | solution.py:466
  57.5 2.4 %shard_map.69 = (f32[27,128,128]{2,1,0:T(8,128)}, bf16[1,2,8,32,128]{4,3,2,1,0:T(8,128)(2,1)}) custom-call(bf16[224,16,128]{2,1,0:T(8,128)(2,1)} %get-tuple-element.6.grad_hbm, bf16[1,2,8,32,128]{4,3,2,1,0:T(8,128)(2,1)} %get-tuple-element.7.down_hbm), custom_call_target="tpu_custom_call" | custom-call | tf_op jit(solution)/shard_map/pallas_call | solution.py:514

commit v5 on v4

--- a/solution.py
+++ b/solution.py
@@ -142,11 +142,10 @@
         remote(video_hbm.at[0, 0], halo.at[1], sent.at[0], near_recv.at[1], left),
         remote(cot_hbm.at[0, 0], cot.at[1], sent.at[0], near_recv.at[2], left),
     ]
-    for copy in near[:2]:
-        copy.start()
     for d in range(1, n_tm):
         remote(gath.at[tm], gath.at[tm], sent.at[4], stage.at[0], at((tm + d) % n_tm, dp)).start()
-    near[2].start()
+    for copy in near:
+        copy.start()
 
     rim = jnp.zeros((width, 3 * chans), BF16)
     for s in range(4):

time: 60 us -> 55.8 us (0.930)
  Pallas kernels: 59.2 us -> 55 us
    pallas_call x1, Pallas kernels: 56.8 us -> 52.6 us  [per_device(): pl.pallas_call(functools.partial(fused, nx, nz, ny, sa, sb), out_shape=(j...]
where the time goes in v5:
time: 55.8 us; the launch traced here: 55.6 us
  Pallas kernels  55 us (99%)
  between operations  0.64 us (1%)
    pallas_call x1, Pallas kernels, per_device(): pl.pallas_call(functools.partial(fused, nx, nz, ny, sa, sb), out_shape=(j...  52.6 us
    pallas_call x1, Pallas kernels, per_device(): pl.pallas_call(widen_result, out_shape=(jax.ShapeDtypeStruct((27, chans,...  2.37 us

profile of v5, /device:TPU:1, one launch (start us, length us, event | category | flops | bytes accessed | tf_op | source)
XLA Modules:
  0.0 55.6 jit_solution(15169694232034909428)
XLA Ops:
  0.6 52.6 %shard_map.68 = (bf16[1,2,8,32,128]{4,3,2,1,0:T(8,128)(2,1)}, bf16[224,16,128]{2,1,0:T(8,128)(2,1)}) custom-call(s32[1,2]{1,0:T(1,128)} %first_hbm.1, f32[1,128]{1,0:T(1,128)} %bitcast.2, bf16[1,2,16,64,128]{4,3,2,1,0:T(8,128)(2,1)} %video_hbm.1, bf16[3,3,3,128,128]{4,3,2,1,0:T(8,128)(2,1)} %kern_hbm.1, bf16[1,2,8,32,128]{4,3,2,1,0:T(8,128)(2,1)} %cot_hbm.1), custom_call_target="tpu_custom_call" | custom-call | tf_op jit(solution)/shard_map/pallas_call | solution.py:465
  53.3 2.4 %shard_map.69 = (f32[27,128,128]{2,1,0:T(8,128)}, bf16[1,2,8,32,128]{4,3,2,1,0:T(8,128)(2,1)}) custom-call(bf16[224,16,128]{2,1,0:T(8,128)(2,1)} %get-tuple-element.6.grad_hbm, bf16[1,2,8,32,128]{4,3,2,1,0:T(8,128)(2,1)} %get-tuple-element.7.down_hbm), custom_call_target="tpu_custom_call" | custom-call | tf_op jit(solution)/shard_map/pallas_call | solution.py:513

commit v6 on v5

--- a/solution.py
+++ b/solution.py
@@ -66,6 +66,7 @@
     pixels = height * width
     n_tm = nx * nz
     n_a = nx * ny * sa
+    za = nx * sa // nz
 
     tm = lax.axis_index("tm")
     dp = lax.axis_index("dp")
@@ -109,9 +110,10 @@
         load.start()
 
     barrier = pltpu.get_barrier_semaphore()
-    peers = [at((tm + d) % n_tm, dp) for d in range(1, n_tm)]
+    peers = [z_peer((z + d) % nz) for d in range(1, nz)]
+    peers += [x_peer((x + d) % nx) for d in range(1, nx)]
     peers += [y_peer((y + d) % ny) for d in range(1, ny)]
-    peers += [sibling]
+    peers += [left, right, sibling]
     for peer in peers:
         pl.semaphore_signal(barrier, inc=1, device_id=peer, device_id_type=pl.DeviceIdType.MESH)
 
@@ -142,8 +144,8 @@
         remote(video_hbm.at[0, 0], halo.at[1], sent.at[0], near_recv.at[1], left),
         remote(cot_hbm.at[0, 0], cot.at[1], sent.at[0], near_recv.at[2], left),
     ]
-    for d in range(1, n_tm):
-        remote(gath.at[tm], gath.at[tm], sent.at[4], stage.at[0], at((tm + d) % n_tm, dp)).start()
+    for d in range(1, nz):
+        remote(gath.at[tm], gath.at[tm], sent.at[4], stage.at[0], z_peer((z + d) % nz)).start()
     for copy in near:
         copy.start()
 
@@ -166,8 +168,13 @@
     loads[3].wait()
     loads[4].wait()
 
-    others = gath.at[pl.ds(0, n_tm - 1)]
+    others = gath.at[pl.ds(0, nz - 1)]
     remote(others, others, sent.at[4], stage.at[0], right).wait_recv()
+    line = gath.at[pl.ds(x * nz, nz)]
+    for d in range(1, nx):
+        remote(line, line, sent.at[4], stage.at[11], x_peer((x + d) % nx)).start()
+    others = gath.at[pl.ds(0, (nx - 1) * nz)]
+    remote(others, others, sent.at[4], stage.at[11], right).wait_recv()
 
     t0 = tm * frames
     t2 = (t0 + 2) % (n_tm * frames)
@@ -334,14 +341,14 @@
 
     arrived(ny, r1a, 1)
     s1a[...] = summed(ny, y, part[pl.ds(y * nx * sa, nx * sa)], r1a)
-    exchange(nx, x, lambda q: s1a.at[pl.ds(q * sa, sa)], r2a, 3, x_peer)
+    exchange(nz, z, lambda q: s1a.at[pl.ds(q * za, za)], r2a, 3, z_peer)
     arrived(nx, r1b, 2)
     s1b[...] = summed(nx, x, part[pl.ds(n_a + x * ny * sb, ny * sb)], r1b)
     exchange(ny, y, lambda q: s1b.at[pl.ds(q * sb, sb)], r2b, 4, y_peer)
 
-    arrived(nx, r2a, 3)
-    s2a[...] = summed(nx, x, s1a[pl.ds(x * sa, sa)], r2a)
-    exchange(nz, z, lambda q: s2a, r3a, 5, z_peer)
+    arrived(nz, r2a, 3)
+    s2a[...] = summed(nz, z, s1a[pl.ds(z * za, za)], r2a)
+    exchange(nx, x, lambda q: s2a, r3a, 5, x_peer)
     arrived(ny, r2b, 4)
     s2b[...] = summed(ny, y, s1b[pl.ds(y * sb, sb)], r2b)
     exchange(nz, z, lambda q: s2b, r3b, 6, z_peer)
@@ -361,10 +368,10 @@
     def some(tiles):
         return full.at[pl.ds(0, tiles)]
 
-    arrived(nz, r3a, 5)
-    a_piece = full.at[pl.ds(base + (y * nx + x) * sa, sa)]
-    a_piece[...] = summed(nz, z, s2a[...], r3a)
-    spread_out(nx, x, a_piece, 2, stage.at[7], x_peer)
+    arrived(nx, r3a, 5)
+    a_piece = full.at[pl.ds(base + y * nx * sa + z * za, za)]
+    a_piece[...] = summed(nx, x, s2a[...], r3a)
+    spread_out(nz, z, a_piece, 2, stage.at[7], z_peer)
     arrived(nz, r3b, 6)
     b_piece = full.at[pl.ds(base + n_a + (x * ny + y) * sb, sb)]
     b_piece[...] = summed(nz, z, s2b[...], r3b)
@@ -376,7 +383,7 @@
     def give_b(q):
         remote(b_line(q), b_line(q), sent.at[3], stage.at[10], sibling).start()
 
-    remote(some((nx - 1) * sa), some((nx - 1) * sa), sent.at[2], stage.at[7], sibling).wait_recv()
+    remote(some((nz - 1) * za), some((nz - 1) * za), sent.at[2], stage.at[7], sibling).wait_recv()
     spread_out(ny, y, a_line(y), 3, line_a.at[y], y_peer)
     give_a(y)
     remote(some((ny - 1) * sb), some((ny - 1) * sb), sent.at[2], stage.at[8], sibling).wait_recv()
@@ -404,9 +411,10 @@
     remote(some(HALF - n_a), some(HALF - n_a), sent.at[3], stage.at[10], sibling).wait_recv()
     writes.append(write(base + n_a, HALF - n_a, 8))
 
+    others = gath.at[pl.ds(0, n_tm - 1)]
     remote(others, others, sent.at[4], stage.at[0], right).wait_send()
     lines = (ny - 1) * nx * sa + (nx - 1) * ny * sb
-    pieces = 2 * ((nx - 1) * sa + (ny - 1) * sb) + (nz - 1) * (sa + sb)
+    pieces = 2 * ((nz - 1) * za + (ny - 1) * sb) + (nx - 1) * za + (nz - 1) * sb
     frames_out = frames * (pixels + half_h * half_w) // 16
     for group, tiles in ((0, frames_out), (1, HALF + lines), (2, pieces), (3, HALF + lines)):
         remote(some(tiles), some(tiles), sent.at[group], stage.at[0], sibling).wait_send()
@@ -491,18 +499,18 @@
             tiles(nx, ny * sb),
             tiles(nx * sa),
             tiles(ny * sb),
-            tiles(nx, sa),
+            tiles(nz, nx * sa // nz),
             tiles(ny, sb),
-            tiles(sa),
+            tiles(nx * sa // nz),
             tiles(sb),
-            tiles(nz, sa),
+            tiles(nx, nx * sa // nz),
             tiles(nz, sb),
             tiles(2 * HALF),
             sem((9,)),
             sem((5,)),
             sem((4,)),
             sem((3,)),
-            sem((11,)),
+            sem((12,)),
             sem((ny,)),
             sem((nx,)),
         ],

time: 55.8 us -> 56.2 us (level)
  no operation moved by 1% of the time
where the time goes in v6:
time: 56.2 us; the launch traced here: 56 us
  Pallas kernels  55.4 us (99%)
  between operations  0.64 us (1%)
    pallas_call x1, Pallas kernels, per_device(): pl.pallas_call(functools.partial(fused, nx, nz, ny, sa, sb), out_shape=(j...  53 us
    pallas_call x1, Pallas kernels, per_device(): pl.pallas_call(widen_result, out_shape=(jax.ShapeDtypeStruct((27, chans,...  2.37 us

profile of v6, /device:TPU:1, one launch (start us, length us, event | category | flops | bytes accessed | tf_op | source)
XLA Modules:
  0.0 56.0 jit_solution(15353655125997030487)
XLA Ops:
  0.6 53.0 %shard_map.68 = (bf16[1,2,8,32,128]{4,3,2,1,0:T(8,128)(2,1)}, bf16[224,16,128]{2,1,0:T(8,128)(2,1)}) custom-call(s32[1,2]{1,0:T(1,128)} %first_hbm.1, f32[1,128]{1,0:T(1,128)} %bitcast.2, bf16[1,2,16,64,128]{4,3,2,1,0:T(8,128)(2,1)} %video_hbm.1, bf16[3,3,3,128,128]{4,3,2,1,0:T(8,128)(2,1)} %kern_hbm.1, bf16[1,2,8,32,128]{4,3,2,1,0:T(8,128)(2,1)} %cot_hbm.1), custom_call_target="tpu_custom_call" | custom-call | tf_op jit(solution)/shard_map/pallas_call | solution.py:473
  53.7 2.4 %shard_map.69 = (f32[27,128,128]{2,1,0:T(8,128)}, bf16[1,2,8,32,128]{4,3,2,1,0:T(8,128)(2,1)}) custom-call(bf16[224,16,128]{2,1,0:T(8,128)(2,1)} %get-tuple-element.6.grad_hbm, bf16[1,2,8,32,128]{4,3,2,1,0:T(8,128)(2,1)} %get-tuple-element.7.down_hbm), custom_call_target="tpu_custom_call" | custom-call | tf_op jit(solution)/shard_map/pallas_call | solution.py:521

commit v7 on v6

--- a/solution.py
+++ b/solution.py
@@ -37,7 +37,7 @@
     spread,
     pool,
     down,
-    dts,
+    dcs,
     gath,
     grads,
     r_pair,
@@ -110,10 +110,9 @@
         load.start()
 
     barrier = pltpu.get_barrier_semaphore()
-    peers = [z_peer((z + d) % nz) for d in range(1, nz)]
-    peers += [x_peer((x + d) % nx) for d in range(1, nx)]
+    peers = [at((tm + d) % n_tm, dp) for d in range(1, n_tm)]
     peers += [y_peer((y + d) % ny) for d in range(1, ny)]
-    peers += [left, right, sibling]
+    peers += [sibling]
     for peer in peers:
         pl.semaphore_signal(barrier, inc=1, device_id=peer, device_id_type=pl.DeviceIdType.MESH)
 
@@ -139,13 +138,20 @@
 
     pl.semaphore_wait(barrier, len(peers))
 
-    near = [
-        remote(video_hbm.at[0, 1], halo.at[0], sent.at[0], near_recv.at[0], right),
-        remote(video_hbm.at[0, 0], halo.at[1], sent.at[0], near_recv.at[1], left),
-        remote(cot_hbm.at[0, 0], cot.at[1], sent.at[0], near_recv.at[2], left),
-    ]
-    for d in range(1, nz):
-        remote(gath.at[tm], gath.at[tm], sent.at[4], stage.at[0], z_peer((z + d) % nz)).start()
+    parts = 4
+    step = height // parts
+    edges = [0] + [c * step + 1 for c in range(1, parts)] + [height]
+    spans = [pl.ds(start, end - start) for start, end in zip(edges[:-1], edges[1:])]
+    near = []
+    for c, span in enumerate(spans):
+        near += [
+            remote(video_hbm.at[0, 1, span], halo.at[0, span], sent.at[0], near_recv.at[2 * c], right),
+            remote(video_hbm.at[0, 0, span], halo.at[1, span], sent.at[0], near_recv.at[2 * c + 1], left),
+        ]
+    near_cot = remote(cot_hbm.at[0, 0], cot.at[1], sent.at[0], near_recv.at[2 * parts], left)
+    for d in range(1, n_tm):
+        remote(gath.at[tm], gath.at[tm], sent.at[4], stage.at[0], at((tm + d) % n_tm, dp)).start()
+    near_cot.start()
     for copy in near:
         copy.start()
 
@@ -168,13 +174,8 @@
     loads[3].wait()
     loads[4].wait()
 
-    others = gath.at[pl.ds(0, nz - 1)]
+    others = gath.at[pl.ds(0, n_tm - 1)]
     remote(others, others, sent.at[4], stage.at[0], right).wait_recv()
-    line = gath.at[pl.ds(x * nz, nz)]
-    for d in range(1, nx):
-        remote(line, line, sent.at[4], stage.at[11], x_peer((x + d) % nx)).start()
-    others = gath.at[pl.ds(0, (nx - 1) * nz)]
-    remote(others, others, sent.at[4], stage.at[11], right).wait_recv()
 
     t0 = tm * frames
     t2 = (t0 + 2) % (n_tm * frames)
@@ -194,8 +195,8 @@
 
     col = lax.broadcasted_iota(jnp.int32, (width, chans), 0)
 
-    def place(source, f, slot, mean, scale, keep):
-        for r in range(height):
+    def place(source, f, slot, mean, scale, keep, span):
+        for r in range(span.start, span.start + span.size):
             value = (source[f, r].astype(F32) - mean) * scale
             if keep is not None:
                 value = jnp.where(keep, value, 0.0)
@@ -213,9 +214,9 @@
     t1_t2 = flag(first2 <= t2 - 1)
     block = min(8, height)
 
-    def patches(slot, r):
-        parts = [xs[slot, r + dy : r + dy + block].reshape(block * width, 3 * chans) for dy in range(3)]
-        return jnp.concatenate(parts, axis=1)
+    def patches(slot, r, rows):
+        shifts = [xs[slot, r + dy : r + dy + rows].reshape(rows * width, 3 * chans) for dy in range(3)]
+        return jnp.concatenate(shifts, axis=1)
 
     def taps(k):
         return kern[k].reshape(9 * chans, chans)
@@ -223,45 +224,48 @@
     def dot(a, b):
         return jnp.dot(a, b, preferred_element_type=F32)
 
-    place(vid, 0, 1, *moments(first0, t0), None)
-    place(vid, 1, 2, *moments(first1, t0 + 1), None)
+    rows = pl.ds(0, height)
+    place(vid, 0, 1, *moments(first0, t0), None, rows)
+    place(vid, 1, 2, *moments(first1, t0 + 1), None, rows)
     for r in range(0, height, block):
         px = pl.ds(r * width, block * width)
-        one = dot(patches(1, r), jnp.concatenate([taps(1), taps(0)], axis=1))
-        two = dot(patches(2, r), jnp.concatenate([taps(2), taps(1)], axis=1))
+        one = dot(patches(1, r, block), jnp.concatenate([taps(1), taps(0)], axis=1))
+        two = dot(patches(2, r, block), jnp.concatenate([taps(2), taps(1)], axis=1))
         acc[0, px] = one[:, :chans] * t0_t1 + two[:, :chans]
         acc[1, px] = one[:, chans:] * t0_t2 + two[:, chans:] * t1_t2
 
     bias = bias_ref[...]
 
-    def finish_conv(f, slot, k):
-        for r in range(0, height, block):
-            last = dot(patches(slot, r), taps(k))
-            for m in range(block // 2):
-                i = r // 2 + m
-                px = slice(i * 2 * width, (i + 1) * 2 * width)
-                value = acc[f, px] + last[m * 2 * width : (m + 1) * 2 * width] + bias
-                logistic = 1.0 / (1.0 + jnp.exp(-value))
-                active = value * logistic
-                pool[f * half_h + i] = active[:width] + active[width:]
-                slope = logistic * (1.0 + value * (1.0 - logistic))
-                over = spread[f * half_h + i]
-                dconv = jnp.concatenate([over, over], axis=0) * slope
-                dts[f * chans : (f + 1) * chans, px] = dconv.T.astype(BF16)
-        for i in range(half_h):
+    def finish_conv(f, slot, k, r):
+        last = dot(patches(slot, r, step), taps(k))
+        for m in range(step // 2):
+            i = r // 2 + m
+            px = slice(i * 2 * width, (i + 1) * 2 * width)
+            value = acc[f, px] + last[m * 2 * width : (m + 1) * 2 * width] + bias
+            logistic = 1.0 / (1.0 + jnp.exp(-value))
+            active = value * logistic
+            pool[f * half_h + i] = active[:width] + active[width:]
+            slope = logistic * (1.0 + value * (1.0 - logistic))
+            over = spread[f * half_h + i]
+            dconv = jnp.concatenate([over, over], axis=0) * slope
+            dcs[px, f * chans : (f + 1) * chans] = dconv.astype(BF16)
+        for i in range(r // 2, (r + step) // 2):
             even = pool[f * half_h + i, pl.ds(0, half_w, stride=2), :]
             odd = pool[f * half_h + i, pl.ds(1, half_w, stride=2), :]
             down[f, i] = ((even + odd) * 0.25).astype(BF16)
 
-    near[0].wait_recv()
-    place(halo, 0, 0, *moments(first1, t0 - 1), first1 <= t0 - 1)
-    finish_conv(0, 0, 0)
-    near[2].wait_recv()
+    earlier = (*moments(first1, t0 - 1), first1 <= t0 - 1)
+    later = (*moments(first2, t2), None)
+    near_cot.wait_recv()
     widen(1)
-    near[1].wait_recv()
-    place(halo, 1, 3, *moments(first2, t2), None)
-    finish_conv(1, 3, 2)
-    out_far = remote(down.at[1], down_hbm.at[0, 0], sent.at[0], near_recv.at[3], right)
+    for c, span in enumerate(spans):
+        near[2 * c].wait_recv()
+        near[2 * c + 1].wait_recv()
+        place(halo, 0, 0, *earlier, span)
+        place(halo, 1, 3, *later, span)
+        finish_conv(0, 0, 0, c * step)
+        finish_conv(1, 3, 2, c * step)
+    out_far = remote(down.at[1], down_hbm.at[0, 0], sent.at[0], near_recv.at[2 * parts + 1], right)
     out_near = pltpu.make_async_copy(down.at[0], down_hbm.at[0, 1], local_sem.at[5])
     out_far.start()
     out_near.start()
@@ -296,19 +300,25 @@
     def a_ready(done):
         return [q for q in range(ny) if (q + 1) * nx * sa <= done]
 
+    def tap_dot(a, b):
+        return lax.dot_general(a, b, (((0,), (0,)), ((), ())), preferred_element_type=F32)
+
     started = []
     for dy in range(3):
         shifted = [xs[s, dy : dy + height].reshape(pixels, 3 * chans) for s in range(4)]
-        both = dts[...]
-        r0 = dot(both[:chans], shifted[0])
-        r1 = dot(both, shifted[1])
-        r2 = dot(both, shifted[2])
-        r3 = dot(both[chans:], shifted[3])
-        m01, m02, m12 = t0_t1[:, 0:1], t0_t2[:, 0:1], t1_t2[:, 0:1]
-        sums = [r0 + r1[chans:] * m02, r1[:chans] * m01 + r2[chans:] * m12, r2[:chans] + r3]
+        both = dcs[...]
+        r0 = tap_dot(shifted[0], both[:, :chans])
+        r1 = tap_dot(shifted[1], both)
+        r2 = tap_dot(shifted[2], both)
+        r3 = tap_dot(shifted[3], both[:, chans:])
+        sums = [
+            r0 + r1[:, chans:] * t0_t2,
+            r1[:, :chans] * t0_t1 + r2[:, chans:] * t1_t2,
+            r2[:, :chans] + r3,
+        ]
         for k in range(3):
             for dx in range(3):
-                tile = sums[k][:, dx * chans : (dx + 1) * chans].T.astype(BF16)
+                tile = sums[k][dx * chans : (dx + 1) * chans].astype(BF16)
                 spot = ((dy * 3 + k) * 3 + dx) * 4
                 for h in range(2):
                     for q in range(4):
@@ -411,7 +421,6 @@
     remote(some(HALF - n_a), some(HALF - n_a), sent.at[3], stage.at[10], sibling).wait_recv()
     writes.append(write(base + n_a, HALF - n_a, 8))
 
-    others = gath.at[pl.ds(0, n_tm - 1)]
     remote(others, others, sent.at[4], stage.at[0], right).wait_send()
     lines = (ny - 1) * nx * sa + (nx - 1) * ny * sb
     pieces = 2 * ((nz - 1) * za + (ny - 1) * sb) + (nx - 1) * za + (nz - 1) * sb
@@ -490,7 +499,7 @@
             pltpu.VMEM((frames * half_h, width, chans), F32),
             pltpu.VMEM((frames * half_h, width, chans), F32),
             pltpu.VMEM((frames, half_h, half_w, chans), BF16),
-            pltpu.VMEM((frames * chans, height * width), BF16),
+            pltpu.VMEM((height * width, frames * chans), BF16),
             pltpu.VMEM((n_tm, 2, chans), F32),
             tiles(2 * HALF),
             tiles(HALF),
@@ -508,7 +517,7 @@
             tiles(2 * HALF),
             sem((9,)),
             sem((5,)),
-            sem((4,)),
+            sem((10,)),
             sem((3,)),
             sem((12,)),
             sem((ny,)),

time: 56.2 us -> 54.3 us (0.966)
  Pallas kernels: 55.4 us -> 53.6 us
    pallas_call x1, Pallas kernels: 53 us -> 51.2 us  [per_device(): pl.pallas_call(functools.partial(fused, nx, nz, ny, sa, sb), out_shape=(j...]
where the time goes in v7:
time: 54.3 us; the launch traced here: 54.2 us
  Pallas kernels  53.6 us (99%)
  between operations  0.64 us (1%)
    pallas_call x1, Pallas kernels, per_device(): pl.pallas_call(functools.partial(fused, nx, nz, ny, sa, sb), out_shape=(j...  51.2 us
    pallas_call x1, Pallas kernels, per_device(): pl.pallas_call(widen_result, out_shape=(jax.ShapeDtypeStruct((27, chans,...  2.37 us

profile of v7, /device:TPU:1, one launch (start us, length us, event | category | flops | bytes accessed | tf_op | source)
XLA Modules:
  0.0 54.2 jit_solution(575706982742452952)
XLA Ops:
  0.6 51.2 %shard_map.68 = (bf16[1,2,8,32,128]{4,3,2,1,0:T(8,128)(2,1)}, bf16[224,16,128]{2,1,0:T(8,128)(2,1)}) custom-call(s32[1,2]{1,0:T(1,128)} %first_hbm.1, f32[1,128]{1,0:T(1,128)} %bitcast.2, bf16[1,2,16,64,128]{4,3,2,1,0:T(8,128)(2,1)} %video_hbm.1, bf16[3,3,3,128,128]{4,3,2,1,0:T(8,128)(2,1)} %kern_hbm.1, bf16[1,2,8,32,128]{4,3,2,1,0:T(8,128)(2,1)} %cot_hbm.1), custom_call_target="tpu_custom_call" | custom-call | tf_op jit(solution)/shard_map/pallas_call | solution.py:482
  51.8 2.4 %shard_map.69 = (f32[27,128,128]{2,1,0:T(8,128)}, bf16[1,2,8,32,128]{4,3,2,1,0:T(8,128)(2,1)}) custom-call(bf16[224,16,128]{2,1,0:T(8,128)(2,1)} %get-tuple-element.6.grad_hbm, bf16[1,2,8,32,128]{4,3,2,1,0:T(8,128)(2,1)} %get-tuple-element.7.down_hbm), custom_call_target="tpu_custom_call" | custom-call | tf_op jit(solution)/shard_map/pallas_call | solution.py:530

commit v8 on v7

--- a/solution.py
+++ b/solution.py
@@ -60,6 +60,7 @@
     stage,
     line_a,
     line_b,
+    lines_out,
 ):
     _, frames, height, width, chans = video_hbm.shape
     half_h, half_w = height // 2, width // 2
@@ -84,6 +85,9 @@
 
     def z_peer(q):
         return at(x * nz + q, dp)
+
+    def far_first(n):
+        return sorted(range(1, n), key=lambda d: -min(d, n - d))
 
     sibling = at(tm, y * 2 + 1 - core)
     right = at((tm + 1) % n_tm, dp)
@@ -335,7 +339,7 @@
     go(first_b, x, range(nx))
 
     def exchange(n, me, src_of, dst, place, peer):
-        for d in range(1, n):
+        for d in far_first(n):
             q = (me + d) % n
             remote(src_of(q), dst.at[me], sent.at[2], stage.at[place], peer(q)).start()
 
@@ -372,7 +376,7 @@
         return full.at[pl.ds(start + n_a + q * ny * sb, ny * sb)]
 
     def spread_out(n, me, piece, group, recv, peer):
-        for d in range(1, n):
+        for d in far_first(n):
             remote(piece, piece, sent.at[group], recv, peer((me + d) % n)).start()
 
     def some(tiles):
@@ -387,11 +391,19 @@
     b_piece[...] = summed(nz, z, s2b[...], r3b)
     spread_out(ny, y, b_piece, 2, stage.at[8], y_peer)
 
+    def give(tiles, place):
+        remote(full.at[tiles], grad_hbm.at[tiles], sent.at[3], stage.at[9], sibling).start()
+        copy = pltpu.make_async_copy(full.at[tiles], grad_hbm.at[tiles], lines_out.at[place])
+        copy.start()
+        writes.append(copy)
+
+    writes = []
+
     def give_a(q):
-        remote(a_line(q), a_line(q), sent.at[3], stage.at[9], sibling).start()
+        give(pl.ds(base + q * nx * sa, nx * sa), len(writes))
 
     def give_b(q):
-        remote(b_line(q), b_line(q), sent.at[3], stage.at[10], sibling).start()
+        give(pl.ds(base + n_a + q * ny * sb, ny * sb), len(writes))
 
     remote(some((nz - 1) * za), some((nz - 1) * za), sent.at[2], stage.at[7], sibling).wait_recv()
     spread_out(ny, y, a_line(y), 3, line_a.at[y], y_peer)
@@ -399,27 +411,14 @@
     remote(some((ny - 1) * sb), some((ny - 1) * sb), sent.at[2], stage.at[8], sibling).wait_recv()
     spread_out(nx, x, b_line(x), 3, line_b.at[x], x_peer)
     give_b(x)
-    for d in range(1, ny):
+    for d in reversed(far_first(ny)):
         q = (y + ny - d) % ny
         remote(a_line(q), a_line(q), sent.at[3], line_a.at[q], sibling).wait_recv()
         give_a(q)
-    for d in range(1, nx):
+    for d in reversed(far_first(nx)):
         q = (x + nx - d) % nx
         remote(b_line(q), b_line(q), sent.at[3], line_b.at[q], sibling).wait_recv()
         give_b(q)
-
-    def write(start, size, place):
-        tiles = pl.ds(start, size)
-        copy = pltpu.make_async_copy(full.at[tiles], grad_hbm.at[tiles], local_sem.at[place])
-        copy.start()
-        return copy
-
-    writes = [write(base, HALF, 6)]
-    base = (1 - core) * HALF
-    remote(some(n_a), some(n_a), sent.at[3], stage.at[9], sibling).wait_recv()
-    writes.append(write(base, n_a, 7))
-    remote(some(HALF - n_a), some(HALF - n_a), sent.at[3], stage.at[10], sibling).wait_recv()
-    writes.append(write(base + n_a, HALF - n_a, 8))
 
     remote(others, others, sent.at[4], stage.at[0], right).wait_send()
     lines = (ny - 1) * nx * sa + (nx - 1) * ny * sb
@@ -428,6 +427,8 @@
     for group, tiles in ((0, frames_out), (1, HALF + lines), (2, pieces), (3, HALF + lines)):
         remote(some(tiles), some(tiles), sent.at[group], stage.at[0], sibling).wait_send()
 
+    theirs = grad_hbm.at[pl.ds((1 - core) * HALF, HALF)]
+    remote(theirs, theirs, sent.at[3], stage.at[9], sibling).wait_recv()
     out_far.wait_recv()
     out_near.wait()
     for copy in writes:
@@ -522,6 +523,7 @@
             sem((12,)),
             sem((ny,)),
             sem((nx,)),
+            sem((ny + nx,)),
         ],
         compiler_params=pltpu.CompilerParams(
             collective_id=0, has_side_effects=True, vmem_limit_bytes=62 * 1024 * 1024

time: 54.3 us -> 53.1 us (0.978)
  Pallas kernels: 53.6 us -> 52.3 us
    pallas_call x1, Pallas kernels: 51.2 us -> 49.9 us  [per_device(): pl.pallas_call(functools.partial(fused, nx, nz, ny, sa, sb), out_shape=(j...]
where the time goes in v8:
time: 53.1 us; the launch traced here: 53 us
  Pallas kernels  52.3 us (98%)
  between operations  0.64 us (1%)
    pallas_call x1, Pallas kernels, per_device(): pl.pallas_call(functools.partial(fused, nx, nz, ny, sa, sb), out_shape=(j...  49.9 us
    pallas_call x1, Pallas kernels, per_device(): pl.pallas_call(widen_result, out_shape=(jax.ShapeDtypeStruct((27, chans,...  2.37 us

profile of v8, /device:TPU:1, one launch (start us, length us, event | category | flops | bytes accessed | tf_op | source)
XLA Modules:
  0.0 53.0 jit_solution(4218529700825432120)
XLA Ops:
  0.6 49.9 %shard_map.68 = (bf16[1,2,8,32,128]{4,3,2,1,0:T(8,128)(2,1)}, bf16[224,16,128]{2,1,0:T(8,128)(2,1)}) custom-call(s32[1,2]{1,0:T(1,128)} %first_hbm.1, f32[1,128]{1,0:T(1,128)} %bitcast.2, bf16[1,2,16,64,128]{4,3,2,1,0:T(8,128)(2,1)} %video_hbm.1, bf16[3,3,3,128,128]{4,3,2,1,0:T(8,128)(2,1)} %kern_hbm.1, bf16[1,2,8,32,128]{4,3,2,1,0:T(8,128)(2,1)} %cot_hbm.1), custom_call_target="tpu_custom_call" | custom-call | tf_op jit(solution)/shard_map/pallas_call | solution.py:483
  50.6 2.4 %shard_map.69 = (f32[27,128,128]{2,1,0:T(8,128)}, bf16[1,2,8,32,128]{4,3,2,1,0:T(8,128)(2,1)}) custom-call(bf16[224,16,128]{2,1,0:T(8,128)(2,1)} %get-tuple-element.6.grad_hbm, bf16[1,2,8,32,128]{4,3,2,1,0:T(8,128)(2,1)} %get-tuple-element.7.down_hbm), custom_call_target="tpu_custom_call" | custom-call | tf_op jit(solution)/shard_map/pallas_call | solution.py:532

commit v9 on v8

--- a/solution.py
+++ b/solution.py
@@ -71,8 +71,8 @@
 
     tm = lax.axis_index("tm")
     dp = lax.axis_index("dp")
-    x, z = tm // nz, tm % nz
-    y, core = dp // 2, dp % 2
+    x, z = lax.div(tm, nz), lax.rem(tm, nz)
+    y, core = lax.div(dp, 2), lax.rem(dp, 2)
 
     def at(tm_to, dp_to):
         return {"tm": tm_to, "dp": dp_to}
@@ -90,8 +90,8 @@
         return sorted(range(1, n), key=lambda d: -min(d, n - d))
 
     sibling = at(tm, y * 2 + 1 - core)
-    right = at((tm + 1) % n_tm, dp)
-    left = at((tm + n_tm - 1) % n_tm, dp)
+    right = at(lax.rem(tm + 1, n_tm), dp)
+    left = at(lax.rem(tm + n_tm - 1, n_tm), dp)
 
     def remote(src, dst, send, recv, to):
         return pltpu.make_async_remote_copy(
@@ -114,8 +114,8 @@
         load.start()
 
     barrier = pltpu.get_barrier_semaphore()
-    peers = [at((tm + d) % n_tm, dp) for d in range(1, n_tm)]
-    peers += [y_peer((y + d) % ny) for d in range(1, ny)]
+    line = [at(lax.rem(tm + d, n_tm), dp) for d in range(1, n_tm)]
+    peers = line + [y_peer(lax.rem(y + d, ny)) for d in range(1, ny)]
     peers += [sibling]
     for peer in peers:
         pl.semaphore_signal(barrier, inc=1, device_id=peer, device_id_type=pl.DeviceIdType.MESH)
@@ -153,11 +153,11 @@
             remote(video_hbm.at[0, 0, span], halo.at[1, span], sent.at[0], near_recv.at[2 * c + 1], left),
         ]
     near_cot = remote(cot_hbm.at[0, 0], cot.at[1], sent.at[0], near_recv.at[2 * parts], left)
-    for d in range(1, n_tm):
-        remote(gath.at[tm], gath.at[tm], sent.at[4], stage.at[0], at((tm + d) % n_tm, dp)).start()
-    near_cot.start()
+    for peer in line:
+        remote(gath.at[tm], gath.at[tm], sent.at[4], stage.at[0], peer).start()
     for copy in near:
         copy.start()
+    near_cot.start()
 
     rim = jnp.zeros((width, 3 * chans), BF16)
     for s in range(4):
@@ -182,8 +182,8 @@
     remote(others, others, sent.at[4], stage.at[0], right).wait_recv()
 
     t0 = tm * frames
-    t2 = (t0 + 2) % (n_tm * frames)
-    first2 = gath[(tm + 1) % n_tm, 1:2].astype(jnp.int32)
+    t2 = lax.rem(t0 + 2, n_tm * frames)
+    first2 = gath[lax.rem(tm + 1, n_tm), 1:2].astype(jnp.int32)
     gathered = gath[...]
     frame = lax.broadcasted_iota(jnp.int32, gathered.shape, 0) * frames
     frame = frame + lax.broadcasted_iota(jnp.int32, gathered.shape, 2) % 4 // 2
@@ -250,9 +250,11 @@
             active = value * logistic
             pool[f * half_h + i] = active[:width] + active[width:]
             slope = logistic * (1.0 + value * (1.0 - logistic))
-            over = spread[f * half_h + i]
-            dconv = jnp.concatenate([over, over], axis=0) * slope
-            dcs[px, f * chans : (f + 1) * chans] = dconv.astype(BF16)
+            if f == 0:
+                over = spread[i]
+                dcs[px, :chans] = (jnp.concatenate([over, over], axis=0) * slope).astype(BF16)
+            else:
+                acc[f, px] = slope
         for i in range(r // 2, (r + step) // 2):
             even = pool[f * half_h + i, pl.ds(0, half_w, stride=2), :]
             odd = pool[f * half_h + i, pl.ds(1, half_w, stride=2), :]
@@ -260,8 +262,6 @@
 
     earlier = (*moments(first1, t0 - 1), first1 <= t0 - 1)
     later = (*moments(first2, t2), None)
-    near_cot.wait_recv()
-    widen(1)
     for c, span in enumerate(spans):
         near[2 * c].wait_recv()
         near[2 * c + 1].wait_recv()
@@ -269,6 +269,13 @@
         place(halo, 1, 3, *later, span)
         finish_conv(0, 0, 0, c * step)
         finish_conv(1, 3, 2, c * step)
+
+    near_cot.wait_recv()
+    widen(1)
+    for i in range(half_h):
+        px = slice(i * 2 * width, (i + 1) * 2 * width)
+        over = spread[half_h + i]
+        dcs[px, chans:] = (jnp.concatenate([over, over], axis=0) * acc[1, px]).astype(BF16)
     out_far = remote(down.at[1], down_hbm.at[0, 0], sent.at[0], near_recv.at[2 * parts + 1], right)
     out_near = pltpu.make_async_copy(down.at[0], down_hbm.at[0, 1], local_sem.at[5])
     out_far.start()
@@ -340,7 +347,7 @@
 
     def exchange(n, me, src_of, dst, place, peer):
         for d in far_first(n):
-            q = (me + d) % n
+            q = lax.rem(me + d, n)
             remote(src_of(q), dst.at[me], sent.at[2], stage.at[place], peer(q)).start()
 
     def arrived(n, dst, place):
@@ -350,7 +357,7 @@
     def summed(n, me, own, dst):
         total = own.astype(F32)
         for d in range(1, n):
-            total = total + dst[(me + n - d) % n].astype(F32)
+            total = total + dst[lax.rem(me + n - d, n)].astype(F32)
         return total.astype(BF16)
 
     arrived(ny, r1a, 1)
@@ -377,7 +384,7 @@
 
     def spread_out(n, me, piece, group, recv, peer):
         for d in far_first(n):
-            remote(piece, piece, sent.at[group], recv, peer((me + d) % n)).start()
+            remote(piece, piece, sent.at[group], recv, peer(lax.rem(me + d, n))).start()
 
     def some(tiles):
         return full.at[pl.ds(0, tiles)]
@@ -412,11 +419,11 @@
     spread_out(nx, x, b_line(x), 3, line_b.at[x], x_peer)
     give_b(x)
     for d in reversed(far_first(ny)):
-        q = (y + ny - d) % ny
+        q = lax.rem(y + ny - d, ny)
         remote(a_line(q), a_line(q), sent.at[3], line_a.at[q], sibling).wait_recv()
         give_a(q)
     for d in reversed(far_first(nx)):
-        q = (x + nx - d) % nx
+        q = lax.rem(x + nx - d, nx)
         remote(b_line(q), b_line(q), sent.at[3], line_b.at[q], sibling).wait_recv()
         give_b(q)
 

time: 53.1 us -> 53 us (level)
  no operation moved by 1% of the time
where the time goes in v9:
time: 53 us; the launch traced here: 52.8 us
  Pallas kernels  52.2 us (98%)
  between operations  0.64 us (1%)
    pallas_call x1, Pallas kernels, per_device(): pl.pallas_call(functools.partial(fused, nx, nz, ny, sa, sb), out_shape=(j...  49.8 us
    pallas_call x1, Pallas kernels, per_device(): pl.pallas_call(widen_result, out_shape=(jax.ShapeDtypeStruct((27, chans,...  2.37 us

profile of v9, /device:TPU:1, one launch (start us, length us, event | category | flops | bytes accessed | tf_op | source)
XLA Modules:
  0.0 52.8 jit_solution(4297143853510449808)
XLA Ops:
  0.6 49.8 %shard_map.68 = (bf16[1,2,8,32,128]{4,3,2,1,0:T(8,128)(2,1)}, bf16[224,16,128]{2,1,0:T(8,128)(2,1)}) custom-call(s32[1,2]{1,0:T(1,128)} %first_hbm.1, f32[1,128]{1,0:T(1,128)} %bitcast.2, bf16[1,2,16,64,128]{4,3,2,1,0:T(8,128)(2,1)} %video_hbm.1, bf16[3,3,3,128,128]{4,3,2,1,0:T(8,128)(2,1)} %kern_hbm.1, bf16[1,2,8,32,128]{4,3,2,1,0:T(8,128)(2,1)} %cot_hbm.1), custom_call_target="tpu_custom_call" | custom-call | tf_op jit(solution)/shard_map/pallas_call | solution.py:490
  50.5 2.4 %shard_map.69 = (f32[27,128,128]{2,1,0:T(8,128)}, bf16[1,2,8,32,128]{4,3,2,1,0:T(8,128)(2,1)}) custom-call(bf16[224,16,128]{2,1,0:T(8,128)(2,1)} %get-tuple-element.6.grad_hbm, bf16[1,2,8,32,128]{4,3,2,1,0:T(8,128)(2,1)} %get-tuple-element.7.down_hbm), custom_call_target="tpu_custom_call" | custom-call | tf_op jit(solution)/shard_map/pallas_call | solution.py:539
